TPU v7x, 256 devices: a whole 4x4x8 slice. The times are simulated.
256 devices in a mesh: video: 16 (over z, core), tm: 4 (over x), height: 4 (over y).
Axes of the slice: x: 4, y: 4, z: 8, core: 2. Of those that a mesh axis runs over, the one named last changes fastest.
Arguments:
- features: bfloat16 [16, 2, 32, 96, 8, 128], P('video', None, 'tm', None, 'height'), may hold values from -6 to 6
- frame_counts: int32 [16], replicated, may hold values from 31 to 64, as said below
- places: int32 [16, 32], replicated, may hold values from 0 to 320, as said below
- gain_one: float32 [96], replicated, may hold values from 0.5 to 2
- gain_two: float32 [96], replicated, may hold values from 0.5 to 2
- conv_one: bfloat16 [3, 3, 3, 96, 96], replicated, may hold values from -0.375 to 0.375
- conv_two: bfloat16 [3, 3, 3, 96, 96], replicated, may hold values from -0.375 to 0.375
- bias_one: float32 [96], replicated, may hold values from -3 to 3
- bias_two: float32 [96], replicated, may hold values from -3 to 3
Outputs:
- scored_frames: bfloat16 [16, 40, 96, 8, 128], P('video', 'tm', None, 'height')
Inputs may be any that keep to these rules, and one draw needn't show every extreme that they name: Video v has ceil(frame_counts[v] / 2) live blocks (blocks g with 2 g < frame_counts[v]), a multiple of 16; together the videos have exactly 272 live blocks. `places`: block g lies on tm index (g // 4) % 4. A live block holds a place below 320, no two live blocks the same; a block that is not live holds 320. Owner o is the device of video index o // 4 and tm index o % 4; a live block goes to an owner of its own tm index. Of the 8 blocks of one video on one tm index, at most 1 live ones have one owner p // 5.
All inputs are finite; a program needn't handle non-finite values.
Results may differ from a plain program's by a relative error of at most 0.008.
Values may be sent and summed in bfloat16 or wider, within the bound.
No kernel may reach another device: no remote copies, remote signals or barrier semaphores. Data moves between devices by JAX's collectives and lax.ppermute only.
A program may use at most 128 MiB of HBM per device.

v0:
```python
import functools

import jax
import jax.numpy as jnp
from jax import lax
from jax.experimental import pallas as pl
from jax.experimental.pallas import tpu as pltpu
from jax.sharding import PartitionSpec as P

EPS = 1e-06
BF = 2
RB = 4
SEG = BF * RB
TAIL = 2 * BF
C = 96
W = 128
TAPS = 3 * C
SLOTS = 5


def activate(values, gain, axis):
    mean_square = jnp.mean(values * values, axis=axis, keepdims=True)
    scaled = values * lax.rsqrt(mean_square + EPS) * gain
    return scaled * (0.5 * jnp.tanh(0.5 * scaled) + 0.5)


def ring(value, axis):
    count = lax.axis_size(axis)
    return lax.ppermute(value, axis, [(i, (i + 1) % count) for i in range(count)])


def neighbours(value, axis):
    return ring(value, axis), lax.ppermute(
        value, axis, [((i + 1) % lax.axis_size(axis), i) for i in range(lax.axis_size(axis))]
    )


def spread(values, masks, stack, row, frame):
    left = pltpu.roll(values, 1, 1) * masks[0]
    right = pltpu.roll(values, W - 1, 1) * masks[1]
    columns = slice(frame * W, (frame + 1) * W)
    for tap, shifted in enumerate((left, values, right)):
        start = row * TAPS + tap * C
        stack[start : start + C, columns] = shifted


def multiply(weights, stack, row, frame):
    total = None
    for tap in range(3):
        window = stack[row * TAPS : (row + 4) * TAPS, (frame + tap) * W : (frame + tap + 2) * W]
        part = jnp.dot(weights[tap], window, preferred_element_type=jnp.float32)
        total = part if total is None else total + part
    return total


def decode_kernel(joined, flags, gain_two, bias_one, bias_two, *rest):
    arrays, rest = rest[:9], rest[9:]
    raw, own, low, high, tail, low_tail, high_tail, *plain = arrays
    boxes, first, second, done, weights_one, weights_two, stores = rest[-7:]
    skip = SEG if joined else 0

    @pl.when(flags[0] > 0)
    def _():
        lane = lax.broadcasted_iota(jnp.int32, (C, W), 1)
        masks = [
            jnp.where(lane == edge, 0.0, 1.0).astype(jnp.bfloat16) for edge in (0, W - 1)
        ]
        past = flags[1] > 0
        above = flags[2] > 0
        below = flags[3] > 0
        zero = jnp.zeros((), jnp.bfloat16)
        pair_weights(plain[0], weights_one)
        for frames, base, start, parts in (
            (TAIL, 0, skip, (tail, low_tail, high_tail)),
            (SEG, TAIL, 0, (own, low, high)),
        ):
            for frame in range(frames):
                for row in range(2):
                    values = parts[0][frame, row]
                    spread(values, masks, first, 2 + row, base + frame)
                    values = jnp.where(above, parts[1][start + frame, row], zero)
                    spread(values, masks, first, row, base + frame)
                    values = jnp.where(below, parts[2][start + frame, row], zero)
                    spread(values, masks, first, 4 + row, base + frame)
        gain = gain_two[...]
        offset = bias_one[...]
        for row in range(0, 4, 2):
            for frame in range(0, SEG + 2, 2):
                total = multiply(weights_one, first, row, frame)
                for k in range(2):
                    for j in range(2):
                        part = total[k * C : (k + 1) * C, j * W : (j + 1) * W] + offset
                        part = part.astype(jnp.bfloat16).astype(jnp.float32)
                        part = activate(part, gain, 0)
                        keep = past if frame < 2 else None
                        side = {0: above, 3: below}.get(row + k)
                        if side is not None:
                            keep = side if keep is None else jnp.logical_and(keep, side)
                        if keep is not None:
                            part = jnp.where(keep, part, 0.0)
                        spread(part.astype(jnp.bfloat16), masks, second, row + k, frame + j)
        pair_weights(plain[1], weights_two)
        offset = bias_two[...]

        def store(block):
            return pltpu.make_async_copy(
                done.at[block], boxes.at[flags[5 + block]], stores.at[block]
            )

        for block in range(RB):
            total = multiply(weights_two, second, 0, block * BF)
            for j in range(BF):
                frame = block * BF + j
                for k in range(2):
                    part = total[k * C : (k + 1) * C, j * W : (j + 1) * W] + offset
                    part = part + raw[frame, k].astype(jnp.float32)
                    part = jnp.where(frame < flags[4], part, 0.0)
                    done[block, j, k] = part.astype(jnp.bfloat16)
            store(block).start()
        for block in range(RB):
            store(block).wait()


def decode(flags, raw, own, sides, tail, tail_sides, weights, vectors, boxes, box_count):
    joined = tail_sides is None
    sides = list(sides) if joined else [*sides, *tail_sides]
    operands = [flags, *vectors, raw, own, *sides[:2], tail, *sides[-2:], *weights]
    specs = [pl.BlockSpec(memory_space=pltpu.SMEM)]
    specs += [pl.BlockSpec(memory_space=pltpu.VMEM)] * (len(operands) - 1)
    aliases = {}
    if boxes is not None:
        aliases = {len(operands): 0}
        operands.append(boxes)
        specs.append(pl.BlockSpec(memory_space=pl.ANY))
    paired = pltpu.VMEM((3, 2 * C, 4 * TAPS), jnp.bfloat16)
    return pl.pallas_call(
        functools.partial(decode_kernel, joined),
        out_shape=jax.ShapeDtypeStruct((box_count, BF, 2, C, W), jnp.bfloat16),
        in_specs=specs,
        out_specs=pl.BlockSpec(memory_space=pl.ANY),
        scratch_shapes=[
            pltpu.VMEM((6 * TAPS, (TAIL + SEG) * W), jnp.bfloat16),
            pltpu.VMEM((4 * TAPS, (2 + SEG) * W), jnp.bfloat16),
            pltpu.VMEM((RB, BF, 2, C, W), jnp.bfloat16),
            paired,
            paired,
            pltpu.SemaphoreType.DMA((RB,)),
        ],
        input_output_aliases=aliases,
        compiler_params=pltpu.CompilerParams(vmem_limit_bytes=32 * 2**20),
        cost_estimate=pl.CostEstimate(flops=6 * 10**9, bytes_accessed=4 * 10**6, transcendentals=0),
        name="decode",
    )(*operands)


def pair_weights(weight, pair):
    pair[:, :C, 3 * TAPS :] = jnp.zeros((3, C, TAPS), jnp.bfloat16)
    pair[:, C:, :TAPS] = jnp.zeros((3, C, TAPS), jnp.bfloat16)
    for tap in range(3):
        for row in range(3):
            for cell in range(3):
                tile = weight[tap, row, cell]
                for k in range(2):
                    start = ((row + k) * 3 + cell) * C
                    pair[tap, k * C : (k + 1) * C, start : start + C] = tile


def local(
    features, frame_counts, places, gain_one, gain_two, conv_one, conv_two, bias_one, bias_two
):
    my_video = lax.axis_index("video")
    my_tm = lax.axis_index("tm")
    my_height = lax.axis_index("height")
    videos = lax.axis_size("video")
    tm_count = lax.axis_size("tm")
    heights = lax.axis_size("height")
    rounds = features.shape[1]

    raw, own = [], []
    for turn in range(rounds):
        raw.append(jnp.swapaxes(features[0, turn], 1, 2))
        values = raw[turn].astype(jnp.float32)
        own.append(activate(values, gain_one[:, None], 2).astype(jnp.bfloat16))
    past_0, past_1 = (ring(value[SEG - TAIL :], "tm") for value in own)
    sides_0 = neighbours(own[0], "height")

    held = lax.dynamic_index_in_dim(
        places.reshape(videos, rounds, tm_count, RB), my_tm, 2, keepdims=False
    )
    mine = lax.dynamic_index_in_dim(held, my_video, 0, keepdims=False)
    count = lax.dynamic_index_in_dim(frame_counts, my_video, 0, keepdims=False)
    owner = mine // (SLOTS * tm_count)
    flags = []
    for turn in range(rounds):
        live = count > turn * tm_count * SEG
        past = jnp.logical_or(turn > 0, my_tm > 0)
        limit = count - (turn * tm_count + my_tm) * SEG
        head = jnp.stack([live, past, my_height > 0, my_height < heights - 1, limit])
        flags.append(jnp.concatenate([head, jnp.minimum(owner[turn], videos - 1)]).astype(jnp.int32))

    wide = [jnp.broadcast_to(v[:, None], (C, W)) for v in (gain_two, bias_one, bias_two)]
    weights = (conv_one, conv_two)
    wanted = (my_video * tm_count + my_tm) * SLOTS + jnp.arange(SLOTS)
    match = (held.reshape(videos, -1)[None] == wanted[:, None, None]).astype(jnp.int32)
    found = jnp.sum(match, axis=(1, 2)) > 0
    source = jnp.sum(match * jnp.arange(videos)[None, :, None], axis=(1, 2))

    past_0, past_1, flags, wide, found, source = lax.optimization_barrier(
        (past_0, past_1, flags, wide, found, source)
    )
    leads = my_tm == 0
    tail_0 = jnp.where(leads, jnp.zeros((), jnp.bfloat16), past_0)
    tail_1 = jnp.where(leads, past_0, past_1)
    tail_sides_0 = neighbours(tail_0, "height")
    ends = [side[-1, -1, -1, -1:] for side in sides_0]
    joined, _ = lax.optimization_barrier((jnp.concatenate([own[1], tail_1]), ends))
    sides_1 = neighbours(joined, "height")
    boxes = decode(
        flags[0], raw[0], own[0], sides_0, tail_0, tail_sides_0, weights, wide, None, videos
    )
    boxes = decode(flags[1], raw[1], own[1], sides_1, tail_1, None, weights, wide, boxes, videos)
    received = lax.all_to_all(boxes, "video", split_axis=0, concat_axis=0, tiled=True)
    chosen = jnp.take(received, source, axis=0, mode="clip")
    chosen = jnp.where(found[:, None, None, None, None], chosen, jnp.zeros((), jnp.bfloat16))
    return jnp.swapaxes(chosen, 2, 3).reshape(1, SLOTS * BF, C, 2, W)


def solution(mesh):
    placed = (P("video", None, "tm", None, "height", None), P(), P(), P(), P(), P(), P(), P(), P())
    return jax.shard_map(
        local,
        mesh=mesh,
        in_specs=placed,
        out_specs=P("video", "tm", None, "height", None),
        check_vma=False,
    )
```

profile of v0, /device:TPU:1, one launch (start us, length us, event | category | flops | bytes accessed | tf_op | source)
XLA Modules:
  0.0 90.2 jit_solution(57540503597034151)
XLA Ops:
  0.0 1.7 %fusion.20 = (bf16[1,1,8,96,2,128]{5,4,3,2,1,0:T(2,128)(2,1)S(1)}, bf16[1,1,8,96,2,128]{5,4,3,2,1,0:T(2,128)(2,1)S(1)}) fusion(bf16[1,2,8,96,2,128]{5,4,3,2,1,0:T(2,128)(2,1)} %param.9), kind=kLoop, calls=%fused_computation.45 | loop fusion | bytes 1572864 | tf_op jit(solution)/shard_map/slice | solution.py:181
  1.7 0.0 copy-start.2
  1.7 0.0 copy-start.7
  1.7 0.0 copy-start.4
  1.8 0.0 copy-start.5
  1.8 0.0 copy-start.6
  1.8 0.2 fusion
  2.0 0.0 copy-done.3
  2.0 0.5 fusion.15
  2.5 2.2 %collective-permute-start.4 = (bf16[8,2,96,128]{3,2,1,0:T(8,128)(2,1)S(1)}, bf16[8,2,96,128]{3,2,1,0:T(8,128)(2,1)S(1)}, u32[]{:S(2)}, u32[]{:S(2)}) collective-permute-start(bf16[8,2,96,128]{3,2,1,0:T(8,128)(2,1)S(1)} %get-tuple-element.32.rest_1_), channel_id=1, source_target_pairs={{0,1},{1,2},{2,3},{3,0},{4,5},{5,6},{6,7},{7,4},{8,9},{9,10},{10,1... | collective-permute-start | bytes 1179656 | tf_op jit(solution)/shard_map/ppermute | solution.py:29
  4.7 1.5 %collective-permute-start.5 = (bf16[8,2,96,128]{3,2,1,0:T(8,128)(2,1)S(1)}, bf16[8,2,96,128]{3,2,1,0:T(8,128)(2,1)S(1)}, u32[]{:S(2)}, u32[]{:S(2)}) collective-permute-start(bf16[8,2,96,128]{3,2,1,0:T(8,128)(2,1)S(1)} %get-tuple-element.32.rest_1_), channel_id=1, source_target_pairs={{1,0},{2,1},{3,2},{0,3},{5,4},{6,5},{7,6},{4,7},{9,8},{10,9},{11,1... | collective-permute-start | bytes 1179656 | tf_op jit(solution)/shard_map/ppermute | solution.py:33
  6.3 1.3 %collective-permute-start = (bf16[4,2,96,128]{3,2,1,0:T(8,128)(2,1)S(1)}, bf16[4,2,96,128]{3,2,1,0:T(8,128)(2,1)S(1)}, u32[]{:S(2)}, u32[]{:S(2)}) collective-permute-start(bf16[4,2,96,128]{3,2,1,0:T(8,128)(2,1)S(1)} %slice.28), channel_id=1, source_target_pairs={{0,4},{4,8},{8,12},{12,0},{1,5},{5,9},{9,13},{13,1},{2,6},{6,10},{... | collective-permute-start | bytes 589832 | tf_op jit(solution)/shard_map/ppermute | solution.py:29
  7.6 1.3 %collective-permute-start.1 = (bf16[4,2,96,128]{3,2,1,0:T(8,128)(2,1)S(1)}, bf16[4,2,96,128]{3,2,1,0:T(8,128)(2,1)S(1)}, u32[]{:S(2)}, u32[]{:S(2)}) collective-permute-start(bf16[4,2,96,128]{3,2,1,0:T(8,128)(2,1)S(1)} %slice.29), channel_id=1, source_target_pairs={{0,4},{4,8},{8,12},{12,0},{1,5},{5,9},{9,13},{13,1},{2,6},{6,10},{... | collective-permute-start | bytes 589832 | tf_op jit(solution)/shard_map/ppermute | solution.py:29
  8.9 0.1 copy.29
  9.0 0.2 divide_reduce_fusion
  9.2 0.2 fusion.19
  9.5 0.0 copy-done.7
  9.5 0.6 dynamic_slice.12
  12.7 0.3 fusion.17
  13.0 0.1 concatenate.9.flags
  13.1 0.1 concatenate.10.flags
  13.2 0.0 collective-permute-done
  13.2 2.1 %collective-permute-done.1 = bf16[4,2,96,128]{3,2,1,0:T(8,128)(2,1)S(1)} collective-permute-done((bf16[4,2,96,128]{3,2,1,0:T(8,128)(2,1)S(1)}, bf16[4,2,96,128]{3,2,1,0:T(8,128)(2,1)S(1)}, u32[]{:S(2)}, u32[]{:S(2)}) %collective-permute-start.1) | collective-permute-done | bytes 196640 | tf_op jit(solution)/shard_map/ppermute | solution.py:29
  15.4 0.1 broadcast_in_dim.22.gain_two
  15.4 0.1 broadcast_in_dim.23.bias_one
  15.5 0.1 broadcast_in_dim.24.bias_two
  15.6 0.0 copy-start
  15.7 0.0 copy-start.1
  15.7 1.4 %collective-permute-start.6 = (bf16[4,2,96,128]{3,2,1,0:T(8,128)(2,1)S(1)}, bf16[4,2,96,128]{3,2,1,0:T(8,128)(2,1)S(1)}, u32[]{:S(2)}, u32[]{:S(2)}) collective-permute-start(bf16[4,2,96,128]{3,2,1,0:T(8,128)(2,1)S(1)} %get-tuple-element.27.rest_4_), channel_id=1, source_target_pairs={{0,1},{1,2},{2,3},{3,0},{4,5},{5,6},{6,7},{7,4},{8,9},{9,10},{10,1... | collective-permute-start | bytes 589832 | tf_op jit(solution)/shard_map/ppermute | solution.py:29
  17.0 1.8 %collective-permute-start.7 = (bf16[4,2,96,128]{3,2,1,0:T(8,128)(2,1)S(1)}, bf16[4,2,96,128]{3,2,1,0:T(8,128)(2,1)S(1)}, u32[]{:S(2)}, u32[]{:S(2)}) collective-permute-start(bf16[4,2,96,128]{3,2,1,0:T(8,128)(2,1)S(1)} %get-tuple-element.27.rest_4_), channel_id=1, source_target_pairs={{1,0},{2,1},{3,2},{0,3},{5,4},{6,5},{7,6},{4,7},{9,8},{10,9},{11,1... | collective-permute-start | bytes 589832 | tf_op jit(solution)/shard_map/ppermute | solution.py:33
  18.8 0.1 pad_maximum_fusion
  18.9 0.1 collective-permute-start.2
  18.9 2.8 %collective-permute-done.6.rest_5_ = bf16[4,2,96,128]{3,2,1,0:T(8,128)(2,1)S(1)} collective-permute-done((bf16[4,2,96,128]{3,2,1,0:T(8,128)(2,1)S(1)}, bf16[4,2,96,128]{3,2,1,0:T(8,128)(2,1)S(1)}, u32[]{:S(2)}, u32[]{:S(2)}) %collective-permute-start.6) | collective-permute-done | bytes 196640 | tf_op jit(solution)/shard_map/ppermute | solution.py:29
  21.8 1.5 %collective-permute-start.3 = (bf16[12,2,96,128]{3,2,1,0:T(8,128)(2,1)S(1)}, bf16[12,2,96,128]{3,2,1,0:T(8,128)(2,1)S(1)}, u32[]{:S(2)}, u32[]{:S(2)}) collective-permute-start(bf16[12,2,96,128]{3,2,1,0:T(8,128)(2,1)S(1)} %pad_maximum_fusion), channel_id=1, source_target_pairs={{1,0},{2,1},{3,2},{0,3},{5,4},{6,5},{7,6},{4,7},{9,8},{10,9},{11,1... | collective-permute-start | bytes 1769480 | tf_op jit(solution)/shard_map/ppermute | solution.py:33
  23.2 0.1 copy.44
  23.3 0.1 copy.43
  23.3 0.0 collective-permute-done.7.rest_6_
  23.4 0.0 collective-permute-done.4.rest_2_
  23.4 0.0 collective-permute-done.5.rest_3_
  23.4 7.7 %decode.2.rest_9_ = bf16[16,2,2,96,128]{4,3,2,1,0:T(8,128)(2,1)} custom-call(s32[9]{0:T(128)S(1)} %concatenate.9.flags, f32[96,128]{1,0:T(8,128)S(1)} %broadcast_in_dim.22.gain_two, f32[96,128]{1,0:T(8,128)S(1)} %broadcast_in_dim.23.bias_one, f32[96,128]{1,0:T(8,128)S(1)} %broadcast_in_dim.24.bias_two, bf16[8,2,96,128]{3,2,1,0:T(8,128)(2,1)S(1)} %bitcast.36, ...), custom_call_target="tpu_custom_call" | custom-call | flops 6000000000 | bytes 4000000 | tf_op jit(solution)/shard_map/decode/pallas_call | solution.py:136
  31.2 3.3 %collective-permute-done.2.rest_2_.rest_5_ = bf16[12,2,96,128]{3,2,1,0:T(8,128)(2,1)S(1)} collective-permute-done((bf16[12,2,96,128]{3,2,1,0:T(8,128)(2,1)S(1)}, bf16[12,2,96,128]{3,2,1,0:T(8,128)(2,1)S(1)}, u32[]{:S(2)}, u32[]{:S(2)}) %collective-permute-start.2) | collective-permute-done | bytes 589856 | tf_op jit(solution)/shard_map/ppermute | solution.py:29
  34.5 0.0 collective-permute-done.3.rest_3_.rest_6_
  34.5 0.6 decode.3
  35.1 14.8 %all-to-all-start = ((bf16[16,2,2,96,128]{4,3,2,1,0:T(8,128)(2,1)}), bf16[16,2,2,96,128]{4,3,2,1,0:T(8,128)(2,1)S(1)}, u32[]{:S(2)}, u32[]{:S(2)}) async-start(bf16[16,2,2,96,128]{4,3,2,1,0:T(8,128)(2,1)} %decode.3), calls=%async_computation | async-start | bytes 3145728 | tf_op jit(solution)/shard_map/all_to_all | solution.py:222
  49.8 38.4 %all-to-all-done = bf16[16,2,2,96,128]{4,3,2,1,0:T(8,128)(2,1)S(1)} async-done(((bf16[16,2,2,96,128]{4,3,2,1,0:T(8,128)(2,1)}), bf16[16,2,2,96,128]{4,3,2,1,0:T(8,128)(2,1)S(1)}, u32[]{:S(2)}, u32[]{:S(2)}) %all-to-all-start) | async-done | bytes 1572896 | tf_op jit(solution)/shard_map/all_to_all | solution.py:222
  88.3 0.6 gather_fusion
  88.9 0.1 broadcast_select_fusion
  89.0 1.2 %copy.30 = bf16[1,10,96,2,128]{4,3,2,1,0:T(2,128)(2,1)} copy(bf16[1,10,96,2,128]{4,2,3,1,0:T(8,128)(2,1)S(1)} %bitcast.37) | data formatting | bytes 983040 | tf_op jit(solution)/shard_map/reshape | solution.py:225
  (18 shorter events, 0.1 us)
Async XLA Ops:
  0.0 2.0 %copy-start.3 = (f32[96]{0:T(128)S(1)}, f32[96]{0:T(128)}, u32[]{:S(2)}) copy-start(f32[96]{0:T(128)} %param.12) | copy-start | bytes 1156
  1.7 7.2 %copy-start.2 = (s32[16,32]{1,0:T(8,128)S(1)}, s32[16,32]{1,0:T(8,128)}, u32[]{:S(2)}) copy-start(s32[16,32]{1,0:T(8,128)} %param.11) | copy-start | bytes 6148
  1.7 7.8 %copy-start.7 = (s32[16]{0:T(128)S(1)}, s32[16]{0:T(128)}, u32[]{:S(2)}) copy-start(s32[16]{0:T(128)} %param.10) | copy-start | bytes 196
  1.7 13.6 %copy-start.4 = (f32[96]{0:T(128)S(1)}, f32[96]{0:T(128)}, u32[]{:S(2)}) copy-start(f32[96]{0:T(128)} %param.13) | copy-start | bytes 1156
  1.8 13.7 %copy-start.5 = (f32[96]{0:T(128)S(1)}, f32[96]{0:T(128)}, u32[]{:S(2)}) copy-start(f32[96]{0:T(128)} %param.16) | copy-start | bytes 1156
  1.8 13.8 %copy-start.6 = (f32[96]{0:T(128)S(1)}, f32[96]{0:T(128)}, u32[]{:S(2)}) copy-start(f32[96]{0:T(128)} %param.17) | copy-start | bytes 1156
  2.5 20.8 %collective-permute-start.4 = (bf16[8,2,96,128]{3,2,1,0:T(8,128)(2,1)S(1)}, bf16[8,2,96,128]{3,2,1,0:T(8,128)(2,1)S(1)}, u32[]{:S(2)}, u32[]{:S(2)}) collective-permute-start(bf16[8,2,96,128]{3,2,1,0:T(8,128)(2,1)S(1)} %get-tuple-element.32.rest_1_), channel_id=1, source_target_pairs={{0,1},{1,2},{2,3},{3,0},{4,5},{5,6},{6,7},{7,4},{8,9},{9,10},{10,1... | collective-permute-start | bytes 1179656 | tf_op jit(solution)/shard_map/ppermute | solution.py:29
  4.7 18.6 %collective-permute-start.5 = (bf16[8,2,96,128]{3,2,1,0:T(8,128)(2,1)S(1)}, bf16[8,2,96,128]{3,2,1,0:T(8,128)(2,1)S(1)}, u32[]{:S(2)}, u32[]{:S(2)}) collective-permute-start(bf16[8,2,96,128]{3,2,1,0:T(8,128)(2,1)S(1)} %get-tuple-element.32.rest_1_), channel_id=1, source_target_pairs={{1,0},{2,1},{3,2},{0,3},{5,4},{6,5},{7,6},{4,7},{9,8},{10,9},{11,1... | collective-permute-start | bytes 1179656 | tf_op jit(solution)/shard_map/ppermute | solution.py:33
  6.3 6.9 %collective-permute-start = (bf16[4,2,96,128]{3,2,1,0:T(8,128)(2,1)S(1)}, bf16[4,2,96,128]{3,2,1,0:T(8,128)(2,1)S(1)}, u32[]{:S(2)}, u32[]{:S(2)}) collective-permute-start(bf16[4,2,96,128]{3,2,1,0:T(8,128)(2,1)S(1)} %slice.28), channel_id=1, source_target_pairs={{0,4},{4,8},{8,12},{12,0},{1,5},{5,9},{9,13},{13,1},{2,6},{6,10},{... | collective-permute-start | bytes 589832 | tf_op jit(solution)/shard_map/ppermute | solution.py:29
  7.6 7.8 %collective-permute-start.1 = (bf16[4,2,96,128]{3,2,1,0:T(8,128)(2,1)S(1)}, bf16[4,2,96,128]{3,2,1,0:T(8,128)(2,1)S(1)}, u32[]{:S(2)}, u32[]{:S(2)}) collective-permute-start(bf16[4,2,96,128]{3,2,1,0:T(8,128)(2,1)S(1)} %slice.29), channel_id=1, source_target_pairs={{0,4},{4,8},{8,12},{12,0},{1,5},{5,9},{9,13},{13,1},{2,6},{6,10},{... | collective-permute-start | bytes 589832 | tf_op jit(solution)/shard_map/ppermute | solution.py:29
  15.6 7.7 %copy-start = (bf16[3,3,3,96,96]{4,3,2,1,0:T(8,128)(2,1)S(1)}, bf16[3,3,3,96,96]{4,3,2,1,0:T(8,128)(2,1)}, u32[]{:S(2)}) copy-start(bf16[3,3,3,96,96]{4,3,2,1,0:T(8,128)(2,1)} %rest_7_.3) | copy-start | bytes 1492996
  15.7 7.7 %copy-start.1 = (bf16[3,3,3,96,96]{4,3,2,1,0:T(8,128)(2,1)S(1)}, bf16[3,3,3,96,96]{4,3,2,1,0:T(8,128)(2,1)}, u32[]{:S(2)}) copy-start(bf16[3,3,3,96,96]{4,3,2,1,0:T(8,128)(2,1)} %rest_8_.3) | copy-start | bytes 1492996
  15.7 6.1 %collective-permute-start.6 = (bf16[4,2,96,128]{3,2,1,0:T(8,128)(2,1)S(1)}, bf16[4,2,96,128]{3,2,1,0:T(8,128)(2,1)S(1)}, u32[]{:S(2)}, u32[]{:S(2)}) collective-permute-start(bf16[4,2,96,128]{3,2,1,0:T(8,128)(2,1)S(1)} %get-tuple-element.27.rest_4_), channel_id=1, source_target_pairs={{0,1},{1,2},{2,3},{3,0},{4,5},{5,6},{6,7},{7,4},{8,9},{9,10},{10,1... | collective-permute-start | bytes 589832 | tf_op jit(solution)/shard_map/ppermute | solution.py:29
  17.0 6.3 %collective-permute-start.7 = (bf16[4,2,96,128]{3,2,1,0:T(8,128)(2,1)S(1)}, bf16[4,2,96,128]{3,2,1,0:T(8,128)(2,1)S(1)}, u32[]{:S(2)}, u32[]{:S(2)}) collective-permute-start(bf16[4,2,96,128]{3,2,1,0:T(8,128)(2,1)S(1)} %get-tuple-element.27.rest_4_), channel_id=1, source_target_pairs={{1,0},{2,1},{3,2},{0,3},{5,4},{6,5},{7,6},{4,7},{9,8},{10,9},{11,1... | collective-permute-start | bytes 589832 | tf_op jit(solution)/shard_map/ppermute | solution.py:33
  18.9 15.6 %collective-permute-start.2 = (bf16[12,2,96,128]{3,2,1,0:T(8,128)(2,1)S(1)}, bf16[12,2,96,128]{3,2,1,0:T(8,128)(2,1)S(1)}, u32[]{:S(2)}, u32[]{:S(2)}) collective-permute-start(bf16[12,2,96,128]{3,2,1,0:T(8,128)(2,1)S(1)} %pad_maximum_fusion), channel_id=1, source_target_pairs={{0,1},{1,2},{2,3},{3,0},{4,5},{5,6},{6,7},{7,4},{8,9},{9,10},{10,1... | collective-permute-start | bytes 1769480 | tf_op jit(solution)/shard_map/ppermute | solution.py:29
  21.8 12.7 %collective-permute-start.3 = (bf16[12,2,96,128]{3,2,1,0:T(8,128)(2,1)S(1)}, bf16[12,2,96,128]{3,2,1,0:T(8,128)(2,1)S(1)}, u32[]{:S(2)}, u32[]{:S(2)}) collective-permute-start(bf16[12,2,96,128]{3,2,1,0:T(8,128)(2,1)S(1)} %pad_maximum_fusion), channel_id=1, source_target_pairs={{1,0},{2,1},{3,2},{0,3},{5,4},{6,5},{7,6},{4,7},{9,8},{10,9},{11,1... | collective-permute-start | bytes 1769480 | tf_op jit(solution)/shard_map/ppermute | solution.py:33
  35.1 53.2 %all-to-all-start = ((bf16[16,2,2,96,128]{4,3,2,1,0:T(8,128)(2,1)}), bf16[16,2,2,96,128]{4,3,2,1,0:T(8,128)(2,1)S(1)}, u32[]{:S(2)}, u32[]{:S(2)}) async-start(bf16[16,2,2,96,128]{4,3,2,1,0:T(8,128)(2,1)} %decode.3), calls=%async_computation | async-start | bytes 3145728 | tf_op jit(solution)/shard_map/all_to_all | solution.py:222
where the time goes:
time: 92 us; the launch traced here: 90.2 us
  waiting for transfers between devices  46.7 us (51%)
  starting transfers between devices  25.8 us (28%)
  Pallas kernels  8.33 us (9%)
  local copies, waits for them, and re-layouts  4.77 us (5%)
  between operations  2.9 us (3%)
  other arithmetic  1.75 us (2%)
    all_to_all x1, waiting for transfers between devices, local(): lax.all_to_all(boxes, 'video', split_axis=0, concat_axis=0, tiled=True)  38.4 us
    all_to_all x1, starting transfers between devices, local(): lax.all_to_all(boxes, 'video', split_axis=0, concat_axis=0, tiled=True)  14.8 us
    pallas_call x2, Pallas kernels, decode(): pl.pallas_call(functools.partial(decode_kernel, joined), out_shape=jax.Sh...  8.33 us
    ppermute x5, waiting for transfers between devices, ring(): lax.ppermute(value, axis, [(i, (i + 1) % count) for i in range(count)])  8.27 us
    ppermute x5, starting transfers between devices, ring(): lax.ppermute(value, axis, [(i, (i + 1) % count) for i in range(count)])  6.22 us
    ppermute x3, starting transfers between devices, neighbours(): lax.ppermute(value, axis, [((i + 1) % lax.axis_size(axis), i) for i in ra...  4.76 us
  transfers between devices with their start and end apart: 9, of which 4 were waited for; matrix products, arithmetic and copies ran while one was open for 2% of the time, Pallas kernels for 9%

commit v1 on v0

--- a/solution.py
+++ b/solution.py
@@ -1,4 +1,5 @@
 import functools
+import itertools
 
 import jax
 import jax.numpy as jnp
@@ -24,15 +25,17 @@
     return scaled * (0.5 * jnp.tanh(0.5 * scaled) + 0.5)
 
 
-def ring(value, axis):
-    count = lax.axis_size(axis)
-    return lax.ppermute(value, axis, [(i, (i + 1) % count) for i in range(count)])
-
-
-def neighbours(value, axis):
-    return ring(value, axis), lax.ppermute(
-        value, axis, [((i + 1) % lax.axis_size(axis), i) for i in range(lax.axis_size(axis))]
-    )
+def shifted(value, *steps):
+    axes = tuple(axis for axis, _ in steps)
+    sizes = [lax.axis_size(axis) for axis in axes]
+    pairs = []
+    for source in itertools.product(*map(range, sizes)):
+        target = [(at + step) % size for at, (_, step), size in zip(source, steps, sizes)]
+        index = [0, 0]
+        for at, to, size in zip(source, target, sizes):
+            index = [index[0] * size + at, index[1] * size + to]
+        pairs.append(tuple(index))
+    return lax.ppermute(value, axes, pairs)
 
 
 def spread(values, masks, stack, row, frame):
@@ -53,11 +56,10 @@
     return total
 
 
-def decode_kernel(joined, flags, gain_two, bias_one, bias_two, *rest):
-    arrays, rest = rest[:9], rest[9:]
-    raw, own, low, high, tail, low_tail, high_tail, *plain = arrays
+def decode_kernel(turn, flags, gain_two, bias_one, bias_two, *rest):
+    plain, raw, own, low, high = rest[:2], *rest[2:6]
+    tails, earlier_tails = rest[6:9], rest[9:12]
     boxes, first, second, done, weights_one, weights_two, stores = rest[-7:]
-    skip = SEG if joined else 0
 
     @pl.when(flags[0] > 0)
     def _():
@@ -65,23 +67,25 @@
         masks = [
             jnp.where(lane == edge, 0.0, 1.0).astype(jnp.bfloat16) for edge in (0, W - 1)
         ]
-        past = flags[1] > 0
+        leads = flags[1] > 0
         above = flags[2] > 0
         below = flags[3] > 0
         zero = jnp.zeros((), jnp.bfloat16)
         pair_weights(plain[0], weights_one)
-        for frames, base, start, parts in (
-            (TAIL, 0, skip, (tail, low_tail, high_tail)),
-            (SEG, TAIL, 0, (own, low, high)),
-        ):
-            for frame in range(frames):
-                for row in range(2):
-                    values = parts[0][frame, row]
-                    spread(values, masks, first, 2 + row, base + frame)
-                    values = jnp.where(above, parts[1][start + frame, row], zero)
-                    spread(values, masks, first, row, base + frame)
-                    values = jnp.where(below, parts[2][start + frame, row], zero)
-                    spread(values, masks, first, 4 + row, base + frame)
+        for frame in range(TAIL):
+            for row in range(6):
+                values = tails[row // 2][frame, row % 2]
+                other = earlier_tails[row // 2][frame, row % 2] if turn > 0 else zero
+                values = jnp.where(leads, other, values)
+                if row // 2 != 1:
+                    values = jnp.where(above if row < 2 else below, values, zero)
+                spread(values, masks, first, row, frame)
+        for frame in range(SEG):
+            for row in range(6):
+                values = (low, own, high)[row // 2][frame, row % 2]
+                if row // 2 != 1:
+                    values = jnp.where(above if row < 2 else below, values, zero)
+                spread(values, masks, first, row, TAIL + frame)
         gain = gain_two[...]
         offset = bias_one[...]
         for row in range(0, 4, 2):
@@ -92,7 +96,7 @@
                         part = total[k * C : (k + 1) * C, j * W : (j + 1) * W] + offset
                         part = part.astype(jnp.bfloat16).astype(jnp.float32)
                         part = activate(part, gain, 0)
-                        keep = past if frame < 2 else None
+                        keep = jnp.logical_not(leads) if turn == 0 and frame < 2 else None
                         side = {0: above, 3: below}.get(row + k)
                         if side is not None:
                             keep = side if keep is None else jnp.logical_and(keep, side)
@@ -121,10 +125,8 @@
             store(block).wait()
 
 
-def decode(flags, raw, own, sides, tail, tail_sides, weights, vectors, boxes, box_count):
-    joined = tail_sides is None
-    sides = list(sides) if joined else [*sides, *tail_sides]
-    operands = [flags, *vectors, raw, own, *sides[:2], tail, *sides[-2:], *weights]
+def decode(turn, flags, vectors, weights, raw, own, sides, tails, boxes, box_count):
+    operands = [flags, *vectors, *weights, raw, own, *sides, *tails]
     specs = [pl.BlockSpec(memory_space=pltpu.SMEM)]
     specs += [pl.BlockSpec(memory_space=pltpu.VMEM)] * (len(operands) - 1)
     aliases = {}
@@ -134,7 +136,7 @@
         specs.append(pl.BlockSpec(memory_space=pl.ANY))
     paired = pltpu.VMEM((3, 2 * C, 4 * TAPS), jnp.bfloat16)
     return pl.pallas_call(
-        functools.partial(decode_kernel, joined),
+        functools.partial(decode_kernel, turn),
         out_shape=jax.ShapeDtypeStruct((box_count, BF, 2, C, W), jnp.bfloat16),
         in_specs=specs,
         out_specs=pl.BlockSpec(memory_space=pl.ANY),
@@ -181,8 +183,17 @@
         raw.append(jnp.swapaxes(features[0, turn], 1, 2))
         values = raw[turn].astype(jnp.float32)
         own.append(activate(values, gain_one[:, None], 2).astype(jnp.bfloat16))
-    past_0, past_1 = (ring(value[SEG - TAIL :], "tm") for value in own)
-    sides_0 = neighbours(own[0], "height")
+    sides, tails = [], []
+    for value in own:
+        end = value[SEG - TAIL :]
+        sides.append([shifted(value, ("height", 1)), shifted(value, ("height", -1))])
+        tails.append(
+            [
+                shifted(end, ("tm", 1), ("height", 1)),
+                shifted(end, ("tm", 1)),
+                shifted(end, ("tm", 1), ("height", -1)),
+            ]
+        )
 
     held = lax.dynamic_index_in_dim(
         places.reshape(videos, rounds, tm_count, RB), my_tm, 2, keepdims=False
@@ -193,9 +204,8 @@
     flags = []
     for turn in range(rounds):
         live = count > turn * tm_count * SEG
-        past = jnp.logical_or(turn > 0, my_tm > 0)
         limit = count - (turn * tm_count + my_tm) * SEG
-        head = jnp.stack([live, past, my_height > 0, my_height < heights - 1, limit])
+        head = jnp.stack([live, my_tm == 0, my_height > 0, my_height < heights - 1, limit])
         flags.append(jnp.concatenate([head, jnp.minimum(owner[turn], videos - 1)]).astype(jnp.int32))
 
     wide = [jnp.broadcast_to(v[:, None], (C, W)) for v in (gain_two, bias_one, bias_two)]
@@ -205,20 +215,12 @@
     found = jnp.sum(match, axis=(1, 2)) > 0
     source = jnp.sum(match * jnp.arange(videos)[None, :, None], axis=(1, 2))
 
-    past_0, past_1, flags, wide, found, source = lax.optimization_barrier(
-        (past_0, past_1, flags, wide, found, source)
-    )
-    leads = my_tm == 0
-    tail_0 = jnp.where(leads, jnp.zeros((), jnp.bfloat16), past_0)
-    tail_1 = jnp.where(leads, past_0, past_1)
-    tail_sides_0 = neighbours(tail_0, "height")
-    ends = [side[-1, -1, -1, -1:] for side in sides_0]
-    joined, _ = lax.optimization_barrier((jnp.concatenate([own[1], tail_1]), ends))
-    sides_1 = neighbours(joined, "height")
-    boxes = decode(
-        flags[0], raw[0], own[0], sides_0, tail_0, tail_sides_0, weights, wide, None, videos
-    )
-    boxes = decode(flags[1], raw[1], own[1], sides_1, tail_1, None, weights, wide, boxes, videos)
+    boxes = None
+    for turn in range(rounds):
+        known = tails[turn] + tails[turn - 1] if turn > 0 else tails[turn]
+        boxes = decode(
+            turn, flags[turn], wide, weights, raw[turn], own[turn], sides[turn], known, boxes, videos
+        )
     received = lax.all_to_all(boxes, "video", split_axis=0, concat_axis=0, tiled=True)
     chosen = jnp.take(received, source, axis=0, mode="clip")
     chosen = jnp.where(found[:, None, None, None, None], chosen, jnp.zeros((), jnp.bfloat16))

time: 92 us -> 95 us (1.033); the launches traced: 90.2 us -> 95.2 us
  starting transfers between devices: 25.8 us -> 29.2 us
  local copies, waits for them, and re-layouts: 4.77 us -> 7.41 us
    ppermute x8 -> x10, starting transfers between devices: 11 us -> 16.3 us  [shifted(): return lax.ppermute(value, axes, pairs)]
    all_to_all x1, starting transfers between devices: 14.8 us -> 12.9 us  [local(): lax.all_to_all(boxes, 'video', split_axis=0, concat_axis=0, tiled=True)]
    slice x2, local copies, waits for them, and re-layouts: 0.03 us -> 1.38 us  [local(): end = value[SEG - TAIL:]]
    transpose x0 -> x1, local copies, waits for them, and re-layouts: none -> 1.31 us  [local(): raw.append(jnp.swapaxes(features[0, turn], 1, 2))]
    ppermute x8 -> x10, waiting for transfers between devices: 8.28 us -> 7.88 us  [shifted(): return lax.ppermute(value, axes, pairs)]
  transfers between devices with their start and end apart: 9 -> 11, of which waited for: 4 -> 5; matrix products, arithmetic and copies ran while one was open for 2% -> 4% of each run, Pallas kernels for 9% -> 8%
where the time goes in v1:
time: 95 us; the launch traced here: 95.2 us
  waiting for transfers between devices  45.9 us (48%)
  starting transfers between devices  29.2 us (31%)
  Pallas kernels  8.21 us (9%)
  local copies, waits for them, and re-layouts  7.41 us (8%)
  between operations  2.77 us (3%)
  other arithmetic  1.66 us (2%)
    all_to_all x1, waiting for transfers between devices, local(): lax.all_to_all(boxes, 'video', split_axis=0, concat_axis=0, tiled=True)  38 us
    ppermute x10, starting transfers between devices, shifted(): return lax.ppermute(value, axes, pairs)  16.3 us
    all_to_all x1, starting transfers between devices, local(): lax.all_to_all(boxes, 'video', split_axis=0, concat_axis=0, tiled=True)  12.9 us
    pallas_call x2, Pallas kernels, decode(): pl.pallas_call(functools.partial(decode_kernel, turn), out_shape=jax.Shap...  8.21 us
    ppermute x10, waiting for transfers between devices, shifted(): return lax.ppermute(value, axes, pairs)  7.88 us
  transfers between devices with their start and end apart: 11, of which 5 were waited for; matrix products, arithmetic and copies ran while one was open for 4% of the time, Pallas kernels for 8%

profile of v1, /device:TPU:1, one launch (start us, length us, event | category | flops | bytes accessed | tf_op | source)
XLA Modules:
  0.0 95.2 jit_solution(11099048658390073263)
XLA Ops:
  0.0 1.7 %fusion.20 = (bf16[1,1,8,96,2,128]{5,4,3,2,1,0:T(2,128)(2,1)S(1)}, bf16[1,1,8,96,2,128]{5,4,3,2,1,0:T(2,128)(2,1)S(1)}) fusion(bf16[1,2,8,96,2,128]{5,4,3,2,1,0:T(2,128)(2,1)} %param.9), kind=kLoop, calls=%fused_computation.42 | loop fusion | bytes 1572864 | tf_op jit(solution)/shard_map/slice | solution.py:183
  1.7 0.0 copy-start.2
  1.7 0.0 copy-start.5
  1.7 0.0 copy-start.10
  1.8 0.2 fusion
  2.0 0.5 fusion.15
  2.5 0.0 copy-start.7
  2.5 0.0 copy-start.8
  2.6 0.0 copy-start.9
  2.6 0.0 copy-start
  2.6 0.0 copy-start.1
  2.6 0.7 slice.27
  3.3 4.5 %collective-permute-start.7 = (bf16[4,2,96,128]{3,2,1,0:T(8,128)(2,1)}, bf16[4,2,96,128]{3,2,1,0:T(8,128)(2,1)S(1)}, u32[]{:S(2)}, u32[]{:S(2)}) collective-permute-start(bf16[4,2,96,128]{3,2,1,0:T(8,128)(2,1)} %slice.27), channel_id=1, source_target_pairs={{0,7},{1,4},{2,5},{3,6},{4,11},{5,8},{6,9},{7,10},{8,15},{9,12},{1... | collective-permute-start | bytes 589832 | tf_op jit(solution)/shard_map/ppermute | solution.py:38
  7.8 1.2 %collective-permute-start.6 = (bf16[4,2,96,128]{3,2,1,0:T(8,128)(2,1)}, bf16[4,2,96,128]{3,2,1,0:T(8,128)(2,1)S(1)}, u32[]{:S(2)}, u32[]{:S(2)}) collective-permute-start(bf16[4,2,96,128]{3,2,1,0:T(8,128)(2,1)} %slice.27), channel_id=1, source_target_pairs={{0,4},{4,8},{8,12},{12,0},{1,5},{5,9},{9,13},{13,1},{2,6},{6,10},{... | collective-permute-start | bytes 589832 | tf_op jit(solution)/shard_map/ppermute | solution.py:38
  9.0 0.0 collective-permute-start.5
  9.0 3.3 %collective-permute-start.9 = (bf16[8,2,96,128]{3,2,1,0:T(8,128)(2,1)S(1)}, bf16[8,2,96,128]{3,2,1,0:T(8,128)(2,1)S(1)}, u32[]{:S(2)}, u32[]{:S(2)}) collective-permute-start(bf16[8,2,96,128]{3,2,1,0:T(8,128)(2,1)S(1)} %get-tuple-element.11.rest_3_), channel_id=1, source_target_pairs={{0,3},{1,0},{2,1},{3,2},{4,7},{5,4},{6,5},{7,6},{8,11},{9,8},{10,9... | collective-permute-start | bytes 1179656 | tf_op jit(solution)/shard_map/ppermute | solution.py:38
  12.3 0.0 collective-permute-start.8
  12.3 0.1 copy.27
  12.4 0.2 fusion.19
  12.6 0.2 divide_reduce_fusion
  12.8 0.7 dynamic_slice.13
  16.0 0.7 slice.26
  16.7 0.1 concatenate.6.flags
  16.8 0.1 concatenate.7.flags
  16.9 1.3 %copy_bitcast_fusion = (bf16[8,2,96,128]{3,2,1,0:T(8,128)(2,1)S(1)}, bf16[8,2,96,128]{3,2,1,0:T(8,128)(2,1)S(1)}) fusion(bf16[1,1,8,96,2,128]{5,4,3,2,1,0:T(2,128)(2,1)} %copy-done.2, bf16[1,1,8,96,2,128]{5,4,3,2,1,0:T(2,128)(2,1)} %copy-done.3), kind=kLoop, calls=%fused_computation.22 | loop fusion | bytes 1572864 | tf_op jit(solution)/shard_map/transpose | solution.py:183
  18.2 0.0 collective-permute-done.7.rest_8_.rest_11_
  18.2 2.7 %collective-permute-start.4 = (bf16[4,2,96,128]{3,2,1,0:T(8,128)(2,1)S(1)}, bf16[4,2,96,128]{3,2,1,0:T(8,128)(2,1)S(1)}, u32[]{:S(2)}, u32[]{:S(2)}) collective-permute-start(bf16[4,2,96,128]{3,2,1,0:T(8,128)(2,1)S(1)} %copy-done.4), channel_id=1, source_target_pairs={{0,7},{1,4},{2,5},{3,6},{4,11},{5,8},{6,9},{7,10},{8,15},{9,12},{1... | collective-permute-start | bytes 589832 | tf_op jit(solution)/shard_map/ppermute | solution.py:38
  20.9 0.0 collective-permute-done.6.rest_7_.rest_10_
  20.9 1.2 %collective-permute-start.3 = (bf16[4,2,96,128]{3,2,1,0:T(8,128)(2,1)S(1)}, bf16[4,2,96,128]{3,2,1,0:T(8,128)(2,1)S(1)}, u32[]{:S(2)}, u32[]{:S(2)}) collective-permute-start(bf16[4,2,96,128]{3,2,1,0:T(8,128)(2,1)S(1)} %copy-done.4), channel_id=1, source_target_pairs={{0,4},{4,8},{8,12},{12,0},{1,5},{5,9},{9,13},{13,1},{2,6},{6,10},{... | collective-permute-start | bytes 589832 | tf_op jit(solution)/shard_map/ppermute | solution.py:38
  22.1 0.2 collective-permute-done.5.rest_6_.rest_9_
  22.4 0.8 collective-permute-start.2
  23.1 0.0 collective-permute-done.9.rest_5_
  23.1 2.6 %collective-permute-start.1 = (bf16[8,2,96,128]{3,2,1,0:T(8,128)(2,1)S(1)}, bf16[8,2,96,128]{3,2,1,0:T(8,128)(2,1)S(1)}, u32[]{:S(2)}, u32[]{:S(2)}) collective-permute-start(bf16[8,2,96,128]{3,2,1,0:T(8,128)(2,1)S(1)} %get-tuple-element.12.rest_3_), channel_id=1, source_target_pairs={{0,3},{1,0},{2,1},{3,2},{4,7},{5,4},{6,5},{7,6},{8,11},{9,8},{10,9... | collective-permute-start | bytes 1179656 | tf_op jit(solution)/shard_map/ppermute | solution.py:38
  25.7 1.0 %collective-permute-done.8.rest_4_ = bf16[8,2,96,128]{3,2,1,0:T(8,128)(2,1)S(1)} collective-permute-done((bf16[8,2,96,128]{3,2,1,0:T(8,128)(2,1)S(1)}, bf16[8,2,96,128]{3,2,1,0:T(8,128)(2,1)S(1)}, u32[]{:S(2)}, u32[]{:S(2)}) %collective-permute-start.8) | collective-permute-done | bytes 393248 | tf_op jit(solution)/shard_map/ppermute | solution.py:38
  26.7 0.1 broadcast_in_dim.19.gain_two
  26.8 0.1 broadcast_in_dim.20.bias_one
  26.8 0.1 broadcast_in_dim.21.bias_two
  26.9 0.0 copy-done.1
  26.9 7.6 %decode.2.rest_12_ = bf16[16,2,2,96,128]{4,3,2,1,0:T(8,128)(2,1)} custom-call(s32[9]{0:T(128)S(1)} %concatenate.7.flags, f32[96,128]{1,0:T(8,128)S(1)} %broadcast_in_dim.19.gain_two, f32[96,128]{1,0:T(8,128)S(1)} %broadcast_in_dim.20.bias_one, f32[96,128]{1,0:T(8,128)S(1)} %broadcast_in_dim.21.bias_two, bf16[3,3,3,96,96]{4,3,2,1,0:T(8,128)(2,1)S(1)} %copy-done, ...), custom_call_target="tpu_custom_call" | custom-call | flops 6000000000 | bytes 4000000 | tf_op jit(solution)/shard_map/decode/pallas_call | solution.py:138
  34.6 0.4 collective-permute-done.1.rest_5_
  35.0 6.3 %collective-permute-done.rest_4_ = bf16[8,2,96,128]{3,2,1,0:T(8,128)(2,1)S(1)} collective-permute-done((bf16[8,2,96,128]{3,2,1,0:T(8,128)(2,1)S(1)}, bf16[8,2,96,128]{3,2,1,0:T(8,128)(2,1)S(1)}, u32[]{:S(2)}, u32[]{:S(2)}) %collective-permute-start) | collective-permute-done | bytes 393248 | tf_op jit(solution)/shard_map/ppermute | solution.py:38
  41.3 0.6 decode.3
  41.9 12.9 %all-to-all-start = ((bf16[16,2,2,96,128]{4,3,2,1,0:T(8,128)(2,1)}), bf16[16,2,2,96,128]{4,3,2,1,0:T(8,128)(2,1)S(1)}, u32[]{:S(2)}, u32[]{:S(2)}) async-start(bf16[16,2,2,96,128]{4,3,2,1,0:T(8,128)(2,1)} %decode.3), calls=%async_computation | async-start | bytes 3145728 | tf_op jit(solution)/shard_map/all_to_all | solution.py:224
  54.8 0.3 fusion.16
  55.2 38.0 %all-to-all-done = bf16[16,2,2,96,128]{4,3,2,1,0:T(8,128)(2,1)S(1)} async-done(((bf16[16,2,2,96,128]{4,3,2,1,0:T(8,128)(2,1)}), bf16[16,2,2,96,128]{4,3,2,1,0:T(8,128)(2,1)S(1)}, u32[]{:S(2)}, u32[]{:S(2)}) %all-to-all-start) | async-done | bytes 1572896 | tf_op jit(solution)/shard_map/all_to_all | solution.py:224
  93.2 0.6 gather_fusion
  93.9 0.1 broadcast_select_fusion
  94.0 1.2 %copy.30 = bf16[1,10,96,2,128]{4,3,2,1,0:T(2,128)(2,1)} copy(bf16[1,10,96,2,128]{4,2,3,1,0:T(8,128)(2,1)S(1)} %bitcast.33) | data formatting | bytes 983040 | tf_op jit(solution)/shard_map/reshape | solution.py:227
  (25 shorter events, 0.1 us)
Async XLA Ops:
  0.0 2.0 %copy-start.6 = (f32[96]{0:T(128)S(1)}, f32[96]{0:T(128)}, u32[]{:S(2)}) copy-start(f32[96]{0:T(128)} %param.12) | copy-start | bytes 1156
  1.7 7.3 %copy-start.2 = (bf16[1,1,8,96,2,128]{5,4,3,2,1,0:T(2,128)(2,1)}, bf16[1,1,8,96,2,128]{5,4,3,2,1,0:T(2,128)(2,1)S(1)}, u32[]{:S(2)}) copy-start(bf16[1,1,8,96,2,128]{5,4,3,2,1,0:T(2,128)(2,1)S(1)} %get-tuple-element.7) | copy-start | bytes 1179652
  1.7 7.3 %copy-start.3 = (bf16[1,1,8,96,2,128]{5,4,3,2,1,0:T(2,128)(2,1)}, bf16[1,1,8,96,2,128]{5,4,3,2,1,0:T(2,128)(2,1)S(1)}, u32[]{:S(2)}) copy-start(bf16[1,1,8,96,2,128]{5,4,3,2,1,0:T(2,128)(2,1)S(1)} %get-tuple-element.8) | copy-start | bytes 1179652
  1.7 10.6 %copy-start.5 = (s32[16,32]{1,0:T(8,128)S(1)}, s32[16,32]{1,0:T(8,128)}, u32[]{:S(2)}) copy-start(s32[16,32]{1,0:T(8,128)} %param.11) | copy-start | bytes 6148
  1.7 11.1 %copy-start.10 = (s32[16]{0:T(128)S(1)}, s32[16]{0:T(128)}, u32[]{:S(2)}) copy-start(s32[16]{0:T(128)} %param.10) | copy-start | bytes 196
  2.5 24.2 %copy-start.7 = (f32[96]{0:T(128)S(1)}, f32[96]{0:T(128)}, u32[]{:S(2)}) copy-start(f32[96]{0:T(128)} %param.13) | copy-start | bytes 1156
  2.5 24.2 %copy-start.8 = (f32[96]{0:T(128)S(1)}, f32[96]{0:T(128)}, u32[]{:S(2)}) copy-start(f32[96]{0:T(128)} %param.16) | copy-start | bytes 1156
  2.6 24.3 %copy-start.9 = (f32[96]{0:T(128)S(1)}, f32[96]{0:T(128)}, u32[]{:S(2)}) copy-start(f32[96]{0:T(128)} %param.17) | copy-start | bytes 1156
  2.6 24.4 %copy-start = (bf16[3,3,3,96,96]{4,3,2,1,0:T(8,128)(2,1)S(1)}, bf16[3,3,3,96,96]{4,3,2,1,0:T(8,128)(2,1)}, u32[]{:S(2)}) copy-start(bf16[3,3,3,96,96]{4,3,2,1,0:T(8,128)(2,1)} %rest_0_.3) | copy-start | bytes 1492996
  2.6 24.4 %copy-start.1 = (bf16[3,3,3,96,96]{4,3,2,1,0:T(8,128)(2,1)S(1)}, bf16[3,3,3,96,96]{4,3,2,1,0:T(8,128)(2,1)}, u32[]{:S(2)}) copy-start(bf16[3,3,3,96,96]{4,3,2,1,0:T(8,128)(2,1)} %rest_1_.3) | copy-start | bytes 1492996
  3.3 14.9 %collective-permute-start.7 = (bf16[4,2,96,128]{3,2,1,0:T(8,128)(2,1)}, bf16[4,2,96,128]{3,2,1,0:T(8,128)(2,1)S(1)}, u32[]{:S(2)}, u32[]{:S(2)}) collective-permute-start(bf16[4,2,96,128]{3,2,1,0:T(8,128)(2,1)} %slice.27), channel_id=1, source_target_pairs={{0,7},{1,4},{2,5},{3,6},{4,11},{5,8},{6,9},{7,10},{8,15},{9,12},{1... | collective-permute-start | bytes 589832 | tf_op jit(solution)/shard_map/ppermute | solution.py:38
  7.8 13.1 %collective-permute-start.6 = (bf16[4,2,96,128]{3,2,1,0:T(8,128)(2,1)}, bf16[4,2,96,128]{3,2,1,0:T(8,128)(2,1)S(1)}, u32[]{:S(2)}, u32[]{:S(2)}) collective-permute-start(bf16[4,2,96,128]{3,2,1,0:T(8,128)(2,1)} %slice.27), channel_id=1, source_target_pairs={{0,4},{4,8},{8,12},{12,0},{1,5},{5,9},{9,13},{13,1},{2,6},{6,10},{... | collective-permute-start | bytes 589832 | tf_op jit(solution)/shard_map/ppermute | solution.py:38
  9.0 13.4 %collective-permute-start.5 = (bf16[4,2,96,128]{3,2,1,0:T(8,128)(2,1)}, bf16[4,2,96,128]{3,2,1,0:T(8,128)(2,1)S(1)}, u32[]{:S(2)}, u32[]{:S(2)}) collective-permute-start(bf16[4,2,96,128]{3,2,1,0:T(8,128)(2,1)} %slice.27), channel_id=1, source_target_pairs={{0,5},{1,6},{2,7},{3,4},{4,9},{5,10},{6,11},{7,8},{8,13},{9,14},{1... | collective-permute-start | bytes 589832 | tf_op jit(solution)/shard_map/ppermute | solution.py:38
  9.0 14.1 %collective-permute-start.9 = (bf16[8,2,96,128]{3,2,1,0:T(8,128)(2,1)S(1)}, bf16[8,2,96,128]{3,2,1,0:T(8,128)(2,1)S(1)}, u32[]{:S(2)}, u32[]{:S(2)}) collective-permute-start(bf16[8,2,96,128]{3,2,1,0:T(8,128)(2,1)S(1)} %get-tuple-element.11.rest_3_), channel_id=1, source_target_pairs={{0,3},{1,0},{2,1},{3,2},{4,7},{5,4},{6,5},{7,6},{8,11},{9,8},{10,9... | collective-permute-start | bytes 1179656 | tf_op jit(solution)/shard_map/ppermute | solution.py:38
  12.3 14.4 %collective-permute-start.8 = (bf16[8,2,96,128]{3,2,1,0:T(8,128)(2,1)S(1)}, bf16[8,2,96,128]{3,2,1,0:T(8,128)(2,1)S(1)}, u32[]{:S(2)}, u32[]{:S(2)}) collective-permute-start(bf16[8,2,96,128]{3,2,1,0:T(8,128)(2,1)S(1)} %get-tuple-element.11.rest_3_), channel_id=1, source_target_pairs={{0,1},{1,2},{2,3},{3,0},{4,5},{5,6},{6,7},{7,4},{8,9},{9,10},{10,1... | collective-permute-start | bytes 1179656 | tf_op jit(solution)/shard_map/ppermute | solution.py:38
  16.9 1.3 %copy-start.4 = (bf16[4,2,96,128]{3,2,1,0:T(8,128)(2,1)S(1)}, bf16[4,2,96,128]{3,2,1,0:T(8,128)(2,1)}, u32[]{:S(2)}) copy-start(bf16[4,2,96,128]{3,2,1,0:T(8,128)(2,1)} %slice.26) | copy-start | bytes 589828
  18.2 16.3 %collective-permute-start.4 = (bf16[4,2,96,128]{3,2,1,0:T(8,128)(2,1)S(1)}, bf16[4,2,96,128]{3,2,1,0:T(8,128)(2,1)S(1)}, u32[]{:S(2)}, u32[]{:S(2)}) collective-permute-start(bf16[4,2,96,128]{3,2,1,0:T(8,128)(2,1)S(1)} %copy-done.4), channel_id=1, source_target_pairs={{0,7},{1,4},{2,5},{3,6},{4,11},{5,8},{6,9},{7,10},{8,15},{9,12},{1... | collective-permute-start | bytes 589832 | tf_op jit(solution)/shard_map/ppermute | solution.py:38
  20.9 13.7 %collective-permute-start.3 = (bf16[4,2,96,128]{3,2,1,0:T(8,128)(2,1)S(1)}, bf16[4,2,96,128]{3,2,1,0:T(8,128)(2,1)S(1)}, u32[]{:S(2)}, u32[]{:S(2)}) collective-permute-start(bf16[4,2,96,128]{3,2,1,0:T(8,128)(2,1)S(1)} %copy-done.4), channel_id=1, source_target_pairs={{0,4},{4,8},{8,12},{12,0},{1,5},{5,9},{9,13},{13,1},{2,6},{6,10},{... | collective-permute-start | bytes 589832 | tf_op jit(solution)/shard_map/ppermute | solution.py:38
  22.4 12.3 %collective-permute-start.2 = (bf16[4,2,96,128]{3,2,1,0:T(8,128)(2,1)S(1)}, bf16[4,2,96,128]{3,2,1,0:T(8,128)(2,1)S(1)}, u32[]{:S(2)}, u32[]{:S(2)}) collective-permute-start(bf16[4,2,96,128]{3,2,1,0:T(8,128)(2,1)S(1)} %copy-done.4), channel_id=1, source_target_pairs={{0,5},{1,6},{2,7},{3,4},{4,9},{5,10},{6,11},{7,8},{8,13},{9,14},{1... | collective-permute-start | bytes 589832 | tf_op jit(solution)/shard_map/ppermute | solution.py:38
  23.1 11.9 %collective-permute-start.1 = (bf16[8,2,96,128]{3,2,1,0:T(8,128)(2,1)S(1)}, bf16[8,2,96,128]{3,2,1,0:T(8,128)(2,1)S(1)}, u32[]{:S(2)}, u32[]{:S(2)}) collective-permute-start(bf16[8,2,96,128]{3,2,1,0:T(8,128)(2,1)S(1)} %get-tuple-element.12.rest_3_), channel_id=1, source_target_pairs={{0,3},{1,0},{2,1},{3,2},{4,7},{5,4},{6,5},{7,6},{8,11},{9,8},{10,9... | collective-permute-start | bytes 1179656 | tf_op jit(solution)/shard_map/ppermute | solution.py:38
  26.7 14.6 %collective-permute-start = (bf16[8,2,96,128]{3,2,1,0:T(8,128)(2,1)S(1)}, bf16[8,2,96,128]{3,2,1,0:T(8,128)(2,1)S(1)}, u32[]{:S(2)}, u32[]{:S(2)}) collective-permute-start(bf16[8,2,96,128]{3,2,1,0:T(8,128)(2,1)S(1)} %get-tuple-element.12.rest_3_), channel_id=1, source_target_pairs={{0,1},{1,2},{2,3},{3,0},{4,5},{5,6},{6,7},{7,4},{8,9},{9,10},{10,1... | collective-permute-start | bytes 1179656 | tf_op jit(solution)/shard_map/ppermute | solution.py:38
  41.9 51.4 %all-to-all-start = ((bf16[16,2,2,96,128]{4,3,2,1,0:T(8,128)(2,1)}), bf16[16,2,2,96,128]{4,3,2,1,0:T(8,128)(2,1)S(1)}, u32[]{:S(2)}, u32[]{:S(2)}) async-start(bf16[16,2,2,96,128]{4,3,2,1,0:T(8,128)(2,1)} %decode.3), calls=%async_computation | async-start | bytes 3145728 | tf_op jit(solution)/shard_map/all_to_all | solution.py:224

commit v2 on v0

--- a/solution.py
+++ b/solution.py
@@ -74,13 +74,16 @@
             (TAIL, 0, skip, (tail, low_tail, high_tail)),
             (SEG, TAIL, 0, (own, low, high)),
         ):
+            known = True if joined or base > 0 else past
             for frame in range(frames):
                 for row in range(2):
-                    values = parts[0][frame, row]
+                    values = jnp.where(known, parts[0][frame, row], zero)
                     spread(values, masks, first, 2 + row, base + frame)
-                    values = jnp.where(above, parts[1][start + frame, row], zero)
+                    keep = jnp.logical_and(known, above)
+                    values = jnp.where(keep, parts[1][start + frame, row], zero)
                     spread(values, masks, first, row, base + frame)
-                    values = jnp.where(below, parts[2][start + frame, row], zero)
+                    keep = jnp.logical_and(known, below)
+                    values = jnp.where(keep, parts[2][start + frame, row], zero)
                     spread(values, masks, first, 4 + row, base + frame)
         gain = gain_two[...]
         offset = bias_one[...]
@@ -178,11 +181,15 @@
 
     raw, own = [], []
     for turn in range(rounds):
-        raw.append(jnp.swapaxes(features[0, turn], 1, 2))
+        segment = features[0, turn]
+        if turn > 0:
+            segment, own[0] = lax.optimization_barrier((segment, own[0]))
+        raw.append(jnp.swapaxes(segment, 1, 2))
         values = raw[turn].astype(jnp.float32)
         own.append(activate(values, gain_one[:, None], 2).astype(jnp.bfloat16))
     past_0, past_1 = (ring(value[SEG - TAIL :], "tm") for value in own)
     sides_0 = neighbours(own[0], "height")
+    tail_sides_0 = neighbours(past_0, "height")
 
     held = lax.dynamic_index_in_dim(
         places.reshape(videos, rounds, tm_count, RB), my_tm, 2, keepdims=False
@@ -205,18 +212,11 @@
     found = jnp.sum(match, axis=(1, 2)) > 0
     source = jnp.sum(match * jnp.arange(videos)[None, :, None], axis=(1, 2))
 
-    past_0, past_1, flags, wide, found, source = lax.optimization_barrier(
-        (past_0, past_1, flags, wide, found, source)
-    )
-    leads = my_tm == 0
-    tail_0 = jnp.where(leads, jnp.zeros((), jnp.bfloat16), past_0)
-    tail_1 = jnp.where(leads, past_0, past_1)
-    tail_sides_0 = neighbours(tail_0, "height")
-    ends = [side[-1, -1, -1, -1:] for side in sides_0]
-    joined, _ = lax.optimization_barrier((jnp.concatenate([own[1], tail_1]), ends))
-    sides_1 = neighbours(joined, "height")
+    arrived = jnp.logical_and(*[side[-1, -1, -1, -1] < jnp.inf for side in sides_0])
+    tail_1 = jnp.where(jnp.logical_and(my_tm == 0, arrived), past_0, past_1)
+    sides_1 = neighbours(jnp.concatenate([own[1], tail_1]), "height")
     boxes = decode(
-        flags[0], raw[0], own[0], sides_0, tail_0, tail_sides_0, weights, wide, None, videos
+        flags[0], raw[0], own[0], sides_0, past_0, tail_sides_0, weights, wide, None, videos
     )
     boxes = decode(flags[1], raw[1], own[1], sides_1, tail_1, None, weights, wide, boxes, videos)
     received = lax.all_to_all(boxes, "video", split_axis=0, concat_axis=0, tiled=True)

time: 92 us -> 95.8 us (1.041); the launches traced: 90.2 us -> 97.5 us
  waiting for transfers between devices: 46.7 us -> 40.6 us
  starting transfers between devices: 25.8 us -> 31 us
  local copies, waits for them, and re-layouts: 4.77 us -> 9.39 us
  Pallas kernels: 8.33 us -> 9.74 us
  between operations: 2.9 us -> 4.09 us
    ppermute x5, waiting for transfers between devices: 8.27 us -> 2.59 us  [ring(): lax.ppermute(value, axis, [(i, (i + 1) % count) for i in range(count)])]
    ppermute x3, starting transfers between devices: 4.76 us -> 9.22 us  [neighbours(): lax.ppermute(value, axis, [((i + 1) % lax.axis_size(axis), i) for i in ra...]
    all_to_all x1, starting transfers between devices: 14.8 us -> 19.2 us  [local(): lax.all_to_all(boxes, 'video', split_axis=0, concat_axis=0, tiled=True)]
    ppermute x5, starting transfers between devices: 6.22 us -> 2.58 us  [ring(): lax.ppermute(value, axis, [(i, (i + 1) % count) for i in range(count)])]
    unnamed x19 -> x25, local copies, waits for them, and re-layouts: 0.23 us -> 2.98 us
    slice x1 -> x3, local copies, waits for them, and re-layouts: 1.7 us -> 3.56 us  [the longest x2 1.86 us: local(): side[-1, -1, -1, -1] < jnp.inf]
    pallas_call x2, Pallas kernels: 8.33 us -> 9.74 us  [decode(): pl.pallas_call(functools.partial(decode_kernel, joined), out_shape=jax.Sh...]
  transfers between devices with their start and end apart: 9 -> 9, of which waited for: 4 -> 2; matrix products, arithmetic and copies ran while one was open for 2% -> 6% of each run, Pallas kernels for 9% -> 8%
where the time goes in v2:
time: 95.8 us; the launch traced here: 97.5 us
  waiting for transfers between devices  40.6 us (42%)
  starting transfers between devices  31 us (32%)
  Pallas kernels  9.74 us (10%)
  local copies, waits for them, and re-layouts  9.39 us (10%)
  between operations  4.09 us (4%)
  other arithmetic  2.63 us (3%)
    all_to_all x1, waiting for transfers between devices, local(): lax.all_to_all(boxes, 'video', split_axis=0, concat_axis=0, tiled=True)  38 us
    all_to_all x1, starting transfers between devices, local(): lax.all_to_all(boxes, 'video', split_axis=0, concat_axis=0, tiled=True)  19.2 us
    pallas_call x2, Pallas kernels, decode(): pl.pallas_call(functools.partial(decode_kernel, joined), out_shape=jax.Sh...  9.74 us
    ppermute x3, starting transfers between devices, neighbours(): lax.ppermute(value, axis, [((i + 1) % lax.axis_size(axis), i) for i in ra...  9.22 us
    unnamed x25, local copies, waits for them, and re-layouts  2.98 us
    ppermute x5, waiting for transfers between devices, ring(): lax.ppermute(value, axis, [(i, (i + 1) % count) for i in range(count)])  2.59 us
    ppermute x5, starting transfers between devices, ring(): lax.ppermute(value, axis, [(i, (i + 1) % count) for i in range(count)])  2.58 us
  transfers between devices with their start and end apart: 9, of which 2 were waited for; matrix products, arithmetic and copies ran while one was open for 6% of the time, Pallas kernels for 8%

profile of v2, /device:TPU:1, one launch (start us, length us, event | category | flops | bytes accessed | tf_op | source)
XLA Modules:
  0.0 97.5 jit_solution(10429948283631328578)
XLA Ops:
  0.0 1.7 %fusion.20 = (bf16[1,1,8,96,2,128]{5,4,3,2,1,0:T(2,128)(2,1)S(1)}, bf16[1,1,8,96,2,128]{5,4,3,2,1,0:T(2,128)(2,1)S(1)}) fusion(bf16[1,2,8,96,2,128]{5,4,3,2,1,0:T(2,128)(2,1)} %param.9), kind=kLoop, calls=%fused_computation.44 | loop fusion | bytes 1572864 | tf_op jit(solution)/shard_map/slice | solution.py:184
  1.7 0.0 copy-start.4
  1.7 0.1 copy.40
  1.8 0.0 copy-start.5
  1.8 0.1 fusion
  1.9 0.3 fusion.7.rest_1_
  2.2 3.6 %collective-permute-start.1 = (bf16[8,2,96,128]{3,2,1,0:T(8,128)(2,1)S(1)}, bf16[8,2,96,128]{3,2,1,0:T(8,128)(2,1)S(1)}, u32[]{:S(2)}, u32[]{:S(2)}) collective-permute-start(bf16[8,2,96,128]{3,2,1,0:T(8,128)(2,1)S(1)} %fusion.7.rest_1_), channel_id=1, source_target_pairs={{1,0},{2,1},{3,2},{0,3},{5,4},{6,5},{7,6},{4,7},{9,8},{10,9},{11,1... | collective-permute-start | bytes 1179656 | tf_op jit(solution)/shard_map/ppermute | solution.py:33
  5.9 0.0 collective-permute-start
  5.9 1.3 %collective-permute-start.2 = (bf16[4,2,96,128]{3,2,1,0:T(8,128)(2,1)S(1)}, bf16[4,2,96,128]{3,2,1,0:T(8,128)(2,1)S(1)}, u32[]{:S(2)}, u32[]{:S(2)}) collective-permute-start(bf16[4,2,96,128]{3,2,1,0:T(8,128)(2,1)S(1)} %slice.29), channel_id=1, source_target_pairs={{0,4},{4,8},{8,12},{12,0},{1,5},{5,9},{9,13},{13,1},{2,6},{6,10},{... | collective-permute-start | bytes 589832 | tf_op jit(solution)/shard_map/ppermute | solution.py:29
  7.2 0.1 fusion.8
  7.3 0.3 fusion.15.rest_1_
  7.6 0.0 copy-start.10
  7.6 0.0 copy-start.7
  7.6 0.0 copy-start.8
  7.6 0.0 copy-start.9
  7.6 0.0 copy-start
  7.7 0.0 copy-start.1
  7.7 1.3 %collective-permute-start.3 = (bf16[4,2,96,128]{3,2,1,0:T(8,128)(2,1)S(1)}, bf16[4,2,96,128]{3,2,1,0:T(8,128)(2,1)}, u32[]{:S(2)}, u32[]{:S(2)}) collective-permute-start(bf16[4,2,96,128]{3,2,1,0:T(8,128)(2,1)S(1)} %slice.36), channel_id=1, source_target_pairs={{0,4},{4,8},{8,12},{12,0},{1,5},{5,9},{9,13},{13,1},{2,6},{6,10},{... | collective-permute-start | bytes 589832 | tf_op jit(solution)/shard_map/ppermute | solution.py:29
  9.0 0.1 copy.27
  9.1 0.2 fusion.19
  9.3 0.2 divide_reduce_fusion
  9.5 2.6 %collective-permute-done.2.rest_4_ = bf16[4,2,96,128]{3,2,1,0:T(8,128)(2,1)S(1)} collective-permute-done((bf16[4,2,96,128]{3,2,1,0:T(8,128)(2,1)S(1)}, bf16[4,2,96,128]{3,2,1,0:T(8,128)(2,1)S(1)}, u32[]{:S(2)}, u32[]{:S(2)}) %collective-permute-start.2) | collective-permute-done | bytes 196640 | tf_op jit(solution)/shard_map/ppermute | solution.py:29
  12.1 2.9 %collective-permute-start.7 = (bf16[4,2,96,128]{3,2,1,0:T(8,128)(2,1)S(1)}, bf16[4,2,96,128]{3,2,1,0:T(8,128)(2,1)S(1)}, u32[]{:S(2)}, u32[]{:S(2)}) collective-permute-start(bf16[4,2,96,128]{3,2,1,0:T(8,128)(2,1)S(1)} %collective-permute-done.2.rest_4_), channel_id=1, source_target_pairs={{1,0},{2,1},{3,2},{0,3},{5,4},{6,5},{7,6},{4,7},{9,8},{10,9},{11,1... | collective-permute-start | bytes 589832 | tf_op jit(solution)/shard_map/ppermute | solution.py:33
  15.0 0.0 collective-permute-start.6
  15.0 0.0 collective-permute-done.1.rest_3_
  15.0 0.6 slice.35
  15.6 0.8 copy-done.2
  16.9 0.0 collective-permute-done.rest_2_
  17.0 1.3 %slice.34 = bf16[1,1,1,1]{3,2,1,0:T(2,128)(2,1)} slice(bf16[8,2,96,128]{3,2,1,0:T(8,128)(2,1)} %collective-permute-done.rest_2_), slice={[7:8], [1:2], [95:96], [127:128]} | slice | bytes 4 | tf_op jit(solution)/shard_map/slice | solution.py:215
  18.9 0.9 pad_maximum_fusion
  19.7 2.7 %collective-permute-start.5 = (bf16[12,2,96,128]{3,2,1,0:T(8,128)(2,1)}, bf16[12,2,96,128]{3,2,1,0:T(8,128)(2,1)}, u32[]{:S(2)}, u32[]{:S(2)}) collective-permute-start(bf16[12,2,96,128]{3,2,1,0:T(8,128)(2,1)} %pad_maximum_fusion), channel_id=1, source_target_pairs={{1,0},{2,1},{3,2},{0,3},{5,4},{6,5},{7,6},{4,7},{9,8},{10,9},{11,1... | collective-permute-start | bytes 1769480 | tf_op jit(solution)/shard_map/ppermute | solution.py:33
  22.4 1.1 %copy.39 = bf16[1,1,8,96,2,128]{5,3,4,2,1,0:T(8,128)(2,1)S(1)} copy(bf16[1,1,8,96,2,128]{5,4,3,2,1,0:T(2,128)(2,1)} %copy-done.4) | data formatting | bytes 786432
  23.5 0.6 dynamic_slice.13
  26.7 0.1 concatenate.9.flags
  26.8 0.1 concatenate.11.flags
  26.9 0.1 broadcast_in_dim.19.gain_two
  27.0 0.1 broadcast_in_dim.20.bias_one
  27.0 0.1 broadcast_in_dim.21.bias_two
  27.1 0.0 copy-done.1
  27.1 1.0 %copy-done.3 = bf16[8,2,96,128]{3,2,1,0:T(8,128)(2,1)S(1)} copy-done((bf16[8,2,96,128]{3,2,1,0:T(8,128)(2,1)S(1)}, bf16[8,2,96,128]{3,2,1,0:T(8,128)(2,1)}, u32[]{:S(2)}) %copy-start.3) | copy-done | bytes 393240
  28.1 8.1 %decode.2.rest_9_ = bf16[16,2,2,96,128]{4,3,2,1,0:T(8,128)(2,1)} custom-call(s32[9]{0:T(128)S(1)} %concatenate.11.flags, f32[96,128]{1,0:T(8,128)S(1)} %broadcast_in_dim.19.gain_two, f32[96,128]{1,0:T(8,128)S(1)} %broadcast_in_dim.20.bias_one, f32[96,128]{1,0:T(8,128)S(1)} %broadcast_in_dim.21.bias_two, bf16[8,2,96,128]{3,2,1,0:T(8,128)(2,1)S(1)} %bitcast.36, ...), custom_call_target="tpu_custom_call" | custom-call | flops 6000000000 | bytes 4000000 | tf_op jit(solution)/shard_map/decode/pallas_call | solution.py:139
  36.2 1.7 %decode.3 = bf16[16,2,2,96,128]{4,3,2,1,0:T(8,128)(2,1)} custom-call(s32[9]{0:T(128)S(1)} %concatenate.9.flags, f32[96,128]{1,0:T(8,128)S(1)} %broadcast_in_dim.19.gain_two, f32[96,128]{1,0:T(8,128)S(1)} %broadcast_in_dim.20.bias_one, f32[96,128]{1,0:T(8,128)S(1)} %broadcast_in_dim.21.bias_two, ...), custom_call_target="tpu_custom_call", output_to_operand_aliasing={{}: (13, {})} | custom-call | flops 6000000000 | bytes 4000000 | tf_op jit(solution)/shard_map/decode/pallas_call | solution.py:139
  37.9 19.2 %all-to-all-start = ((bf16[16,2,2,96,128]{4,3,2,1,0:T(8,128)(2,1)}), bf16[16,2,2,96,128]{4,3,2,1,0:T(8,128)(2,1)S(1)}, u32[]{:S(2)}, u32[]{:S(2)}) async-start(bf16[16,2,2,96,128]{4,3,2,1,0:T(8,128)(2,1)} %decode.3), calls=%async_computation | async-start | bytes 3145728 | tf_op jit(solution)/shard_map/all_to_all | solution.py:222
  57.1 0.3 fusion.16
  57.5 38.0 %all-to-all-done = bf16[16,2,2,96,128]{4,3,2,1,0:T(8,128)(2,1)S(1)} async-done(((bf16[16,2,2,96,128]{4,3,2,1,0:T(8,128)(2,1)}), bf16[16,2,2,96,128]{4,3,2,1,0:T(8,128)(2,1)S(1)}, u32[]{:S(2)}, u32[]{:S(2)}) %all-to-all-start) | async-done | bytes 1572896 | tf_op jit(solution)/shard_map/all_to_all | solution.py:222
  95.6 0.6 gather_fusion
  96.2 0.1 broadcast_select_fusion
  96.3 1.2 %copy.30 = bf16[1,10,96,2,128]{4,3,2,1,0:T(2,128)(2,1)} copy(bf16[1,10,96,2,128]{4,2,3,1,0:T(8,128)(2,1)S(1)} %bitcast.37) | data formatting | bytes 983040 | tf_op jit(solution)/shard_map/reshape | solution.py:225
  (28 shorter events, 0.2 us)
Async XLA Ops:
  0.0 1.9 %copy-start.6 = (f32[96]{0:T(128)S(1)}, f32[96]{0:T(128)}, u32[]{:S(2)}) copy-start(f32[96]{0:T(128)} %param.12) | copy-start | bytes 1156
  1.7 5.6 %copy-start.4 = (bf16[1,1,8,96,2,128]{5,4,3,2,1,0:T(2,128)(2,1)}, bf16[1,1,8,96,2,128]{5,4,3,2,1,0:T(2,128)(2,1)S(1)}, u32[]{:S(2)}) copy-start(bf16[1,1,8,96,2,128]{5,4,3,2,1,0:T(2,128)(2,1)S(1)} %get-tuple-element.11) | copy-start | bytes 1179652
  1.8 7.2 %copy-start.5 = (s32[16,32]{1,0:T(8,128)S(1)}, s32[16,32]{1,0:T(8,128)}, u32[]{:S(2)}) copy-start(s32[16,32]{1,0:T(8,128)} %param.11) | copy-start | bytes 6148
  2.2 12.8 %collective-permute-start.1 = (bf16[8,2,96,128]{3,2,1,0:T(8,128)(2,1)S(1)}, bf16[8,2,96,128]{3,2,1,0:T(8,128)(2,1)S(1)}, u32[]{:S(2)}, u32[]{:S(2)}) collective-permute-start(bf16[8,2,96,128]{3,2,1,0:T(8,128)(2,1)S(1)} %fusion.7.rest_1_), channel_id=1, source_target_pairs={{1,0},{2,1},{3,2},{0,3},{5,4},{6,5},{7,6},{4,7},{9,8},{10,9},{11,1... | collective-permute-start | bytes 1179656 | tf_op jit(solution)/shard_map/ppermute | solution.py:33
  5.9 11.1 %collective-permute-start = (bf16[8,2,96,128]{3,2,1,0:T(8,128)(2,1)S(1)}, bf16[8,2,96,128]{3,2,1,0:T(8,128)(2,1)}, u32[]{:S(2)}, u32[]{:S(2)}) collective-permute-start(bf16[8,2,96,128]{3,2,1,0:T(8,128)(2,1)S(1)} %fusion.7.rest_1_), channel_id=1, source_target_pairs={{0,1},{1,2},{2,3},{3,0},{4,5},{5,6},{6,7},{7,4},{8,9},{9,10},{10,1... | collective-permute-start | bytes 1179656 | tf_op jit(solution)/shard_map/ppermute | solution.py:29
  5.9 6.2 %collective-permute-start.2 = (bf16[4,2,96,128]{3,2,1,0:T(8,128)(2,1)S(1)}, bf16[4,2,96,128]{3,2,1,0:T(8,128)(2,1)S(1)}, u32[]{:S(2)}, u32[]{:S(2)}) collective-permute-start(bf16[4,2,96,128]{3,2,1,0:T(8,128)(2,1)S(1)} %slice.29), channel_id=1, source_target_pairs={{0,4},{4,8},{8,12},{12,0},{1,5},{5,9},{9,13},{13,1},{2,6},{6,10},{... | collective-permute-start | bytes 589832 | tf_op jit(solution)/shard_map/ppermute | solution.py:29
  7.6 15.9 %copy-start.10 = (s32[16]{0:T(128)S(1)}, s32[16]{0:T(128)}, u32[]{:S(2)}) copy-start(s32[16]{0:T(128)} %param.10) | copy-start | bytes 196
  7.6 19.3 %copy-start.7 = (f32[96]{0:T(128)S(1)}, f32[96]{0:T(128)}, u32[]{:S(2)}) copy-start(f32[96]{0:T(128)} %param.13) | copy-start | bytes 1156
  7.6 19.3 %copy-start.8 = (f32[96]{0:T(128)S(1)}, f32[96]{0:T(128)}, u32[]{:S(2)}) copy-start(f32[96]{0:T(128)} %param.16) | copy-start | bytes 1156
  7.6 19.4 %copy-start.9 = (f32[96]{0:T(128)S(1)}, f32[96]{0:T(128)}, u32[]{:S(2)}) copy-start(f32[96]{0:T(128)} %param.17) | copy-start | bytes 1156
  7.6 19.5 %copy-start = (bf16[3,3,3,96,96]{4,3,2,1,0:T(8,128)(2,1)S(1)}, bf16[3,3,3,96,96]{4,3,2,1,0:T(8,128)(2,1)}, u32[]{:S(2)}) copy-start(bf16[3,3,3,96,96]{4,3,2,1,0:T(8,128)(2,1)} %rest_7_.3) | copy-start | bytes 1492996
  7.7 19.5 %copy-start.1 = (bf16[3,3,3,96,96]{4,3,2,1,0:T(8,128)(2,1)S(1)}, bf16[3,3,3,96,96]{4,3,2,1,0:T(8,128)(2,1)}, u32[]{:S(2)}) copy-start(bf16[3,3,3,96,96]{4,3,2,1,0:T(8,128)(2,1)} %rest_8_.3) | copy-start | bytes 1492996
  7.7 11.1 %collective-permute-start.3 = (bf16[4,2,96,128]{3,2,1,0:T(8,128)(2,1)S(1)}, bf16[4,2,96,128]{3,2,1,0:T(8,128)(2,1)}, u32[]{:S(2)}, u32[]{:S(2)}) collective-permute-start(bf16[4,2,96,128]{3,2,1,0:T(8,128)(2,1)S(1)} %slice.36), channel_id=1, source_target_pairs={{0,4},{4,8},{8,12},{12,0},{1,5},{5,9},{9,13},{13,1},{2,6},{6,10},{... | collective-permute-start | bytes 589832 | tf_op jit(solution)/shard_map/ppermute | solution.py:29
  12.1 14.8 %collective-permute-start.7 = (bf16[4,2,96,128]{3,2,1,0:T(8,128)(2,1)S(1)}, bf16[4,2,96,128]{3,2,1,0:T(8,128)(2,1)S(1)}, u32[]{:S(2)}, u32[]{:S(2)}) collective-permute-start(bf16[4,2,96,128]{3,2,1,0:T(8,128)(2,1)S(1)} %collective-permute-done.2.rest_4_), channel_id=1, source_target_pairs={{1,0},{2,1},{3,2},{0,3},{5,4},{6,5},{7,6},{4,7},{9,8},{10,9},{11,1... | collective-permute-start | bytes 589832 | tf_op jit(solution)/shard_map/ppermute | solution.py:33
  15.0 11.9 %collective-permute-start.6 = (bf16[4,2,96,128]{3,2,1,0:T(8,128)(2,1)S(1)}, bf16[4,2,96,128]{3,2,1,0:T(8,128)(2,1)}, u32[]{:S(2)}, u32[]{:S(2)}) collective-permute-start(bf16[4,2,96,128]{3,2,1,0:T(8,128)(2,1)S(1)} %collective-permute-done.2.rest_4_), channel_id=1, source_target_pairs={{0,1},{1,2},{2,3},{3,0},{4,5},{5,6},{6,7},{7,4},{8,9},{9,10},{10,1... | collective-permute-start | bytes 589832 | tf_op jit(solution)/shard_map/ppermute | solution.py:29
  15.6 0.8 copy-start.2
  19.7 16.5 %collective-permute-start.5 = (bf16[12,2,96,128]{3,2,1,0:T(8,128)(2,1)}, bf16[12,2,96,128]{3,2,1,0:T(8,128)(2,1)}, u32[]{:S(2)}, u32[]{:S(2)}) collective-permute-start(bf16[12,2,96,128]{3,2,1,0:T(8,128)(2,1)} %pad_maximum_fusion), channel_id=1, source_target_pairs={{1,0},{2,1},{3,2},{0,3},{5,4},{6,5},{7,6},{4,7},{9,8},{10,9},{11,1... | collective-permute-start | bytes 1769480 | tf_op jit(solution)/shard_map/ppermute | solution.py:33
  22.4 13.8 %collective-permute-start.4 = (bf16[12,2,96,128]{3,2,1,0:T(8,128)(2,1)}, bf16[12,2,96,128]{3,2,1,0:T(8,128)(2,1)}, u32[]{:S(2)}, u32[]{:S(2)}) collective-permute-start(bf16[12,2,96,128]{3,2,1,0:T(8,128)(2,1)} %pad_maximum_fusion), channel_id=1, source_target_pairs={{0,1},{1,2},{2,3},{3,0},{4,5},{5,6},{6,7},{7,4},{8,9},{9,10},{10,1... | collective-permute-start | bytes 1769480 | tf_op jit(solution)/shard_map/ppermute | solution.py:29
  27.1 1.0 %copy-start.3 = (bf16[8,2,96,128]{3,2,1,0:T(8,128)(2,1)S(1)}, bf16[8,2,96,128]{3,2,1,0:T(8,128)(2,1)}, u32[]{:S(2)}) copy-start(bf16[8,2,96,128]{3,2,1,0:T(8,128)(2,1)} %copy-done.2) | copy-start | bytes 1179652
  37.9 57.6 %all-to-all-start = ((bf16[16,2,2,96,128]{4,3,2,1,0:T(8,128)(2,1)}), bf16[16,2,2,96,128]{4,3,2,1,0:T(8,128)(2,1)S(1)}, u32[]{:S(2)}, u32[]{:S(2)}) async-start(bf16[16,2,2,96,128]{4,3,2,1,0:T(8,128)(2,1)} %decode.3), calls=%async_computation | async-start | bytes 3145728 | tf_op jit(solution)/shard_map/all_to_all | solution.py:222

commit v3 on v2

--- a/solution.py
+++ b/solution.py
@@ -65,7 +65,7 @@
         masks = [
             jnp.where(lane == edge, 0.0, 1.0).astype(jnp.bfloat16) for edge in (0, W - 1)
         ]
-        past = flags[1] > 0
+        past = True if joined else flags[1] == 0
         above = flags[2] > 0
         below = flags[3] > 0
         zero = jnp.zeros((), jnp.bfloat16)
@@ -74,10 +74,10 @@
             (TAIL, 0, skip, (tail, low_tail, high_tail)),
             (SEG, TAIL, 0, (own, low, high)),
         ):
-            known = True if joined or base > 0 else past
+            known = True if base > 0 else past
             for frame in range(frames):
                 for row in range(2):
-                    values = jnp.where(known, parts[0][frame, row], zero)
+                    values = jnp.where(known, parts[0][start + frame, row], zero)
                     spread(values, masks, first, 2 + row, base + frame)
                     keep = jnp.logical_and(known, above)
                     values = jnp.where(keep, parts[1][start + frame, row], zero)
@@ -168,6 +168,31 @@
                     pair[tap, k * C : (k + 1) * C, start : start + C] = tile
 
 
+def join_kernel(flags, own, last, past, low, high, joined):
+    joined[:SEG] = own[...]
+
+    @pl.when(flags[1] > 0)
+    def _():
+        joined[SEG:] = last[...]
+
+    @pl.when(flags[1] == 0)
+    def _():
+        joined[SEG:] = past[...]
+
+
+def join(flags, own, last, past, sides):
+    operands = (flags, own, last, past, *sides)
+    return pl.pallas_call(
+        join_kernel,
+        out_shape=jax.ShapeDtypeStruct((SEG + TAIL, 2, C, W), jnp.bfloat16),
+        in_specs=[pl.BlockSpec(memory_space=pltpu.SMEM)]
+        + [pl.BlockSpec(memory_space=pltpu.VMEM)] * (len(operands) - 1),
+        out_specs=pl.BlockSpec(memory_space=pltpu.VMEM),
+        compiler_params=pltpu.CompilerParams(vmem_limit_bytes=8 * 2**20),
+        name="join",
+    )(*operands)
+
+
 def local(
     features, frame_counts, places, gain_one, gain_two, conv_one, conv_two, bias_one, bias_two
 ):
@@ -181,15 +206,11 @@
 
     raw, own = [], []
     for turn in range(rounds):
-        segment = features[0, turn]
-        if turn > 0:
-            segment, own[0] = lax.optimization_barrier((segment, own[0]))
-        raw.append(jnp.swapaxes(segment, 1, 2))
+        raw.append(jnp.swapaxes(features[0, turn], 1, 2))
         values = raw[turn].astype(jnp.float32)
         own.append(activate(values, gain_one[:, None], 2).astype(jnp.bfloat16))
     past_0, past_1 = (ring(value[SEG - TAIL :], "tm") for value in own)
     sides_0 = neighbours(own[0], "height")
-    tail_sides_0 = neighbours(past_0, "height")
 
     held = lax.dynamic_index_in_dim(
         places.reshape(videos, rounds, tm_count, RB), my_tm, 2, keepdims=False
@@ -200,9 +221,9 @@
     flags = []
     for turn in range(rounds):
         live = count > turn * tm_count * SEG
-        past = jnp.logical_or(turn > 0, my_tm > 0)
+        leads = my_tm == 0
         limit = count - (turn * tm_count + my_tm) * SEG
-        head = jnp.stack([live, past, my_height > 0, my_height < heights - 1, limit])
+        head = jnp.stack([live, leads, my_height > 0, my_height < heights - 1, limit])
         flags.append(jnp.concatenate([head, jnp.minimum(owner[turn], videos - 1)]).astype(jnp.int32))
 
     wide = [jnp.broadcast_to(v[:, None], (C, W)) for v in (gain_two, bias_one, bias_two)]
@@ -212,13 +233,16 @@
     found = jnp.sum(match, axis=(1, 2)) > 0
     source = jnp.sum(match * jnp.arange(videos)[None, :, None], axis=(1, 2))
 
-    arrived = jnp.logical_and(*[side[-1, -1, -1, -1] < jnp.inf for side in sides_0])
-    tail_1 = jnp.where(jnp.logical_and(my_tm == 0, arrived), past_0, past_1)
-    sides_1 = neighbours(jnp.concatenate([own[1], tail_1]), "height")
+    past_0, flags, wide, found, source = lax.optimization_barrier(
+        (past_0, flags, wide, found, source)
+    )
+    tail_sides_0 = neighbours(past_0, "height")
+    joined = join(flags[1], own[1], past_0, past_1, sides_0)
+    sides_1 = neighbours(joined, "height")
     boxes = decode(
         flags[0], raw[0], own[0], sides_0, past_0, tail_sides_0, weights, wide, None, videos
     )
-    boxes = decode(flags[1], raw[1], own[1], sides_1, tail_1, None, weights, wide, boxes, videos)
+    boxes = decode(flags[1], raw[1], joined, sides_1, joined, None, weights, wide, boxes, videos)
     received = lax.all_to_all(boxes, "video", split_axis=0, concat_axis=0, tiled=True)
     chosen = jnp.take(received, source, axis=0, mode="clip")
     chosen = jnp.where(found[:, None, None, None, None], chosen, jnp.zeros((), jnp.bfloat16))

time: 95.8 us -> 89.7 us (0.936); the launches traced: 97.5 us -> 90.2 us
  local copies, waits for them, and re-layouts: 9.39 us -> 4.78 us
  waiting for transfers between devices: 40.6 us -> 43.6 us
  starting transfers between devices: 31 us -> 28.4 us
  between operations: 4.09 us -> 2.86 us
  other arithmetic: 2.63 us -> 1.66 us
    ppermute x5, starting transfers between devices: 2.58 us -> 5.35 us  [ring(): lax.ppermute(value, axis, [(i, (i + 1) % count) for i in range(count)])]
    ppermute x3, starting transfers between devices: 9.22 us -> 6.46 us  [neighbours(): lax.ppermute(value, axis, [((i + 1) % lax.axis_size(axis), i) for i in ra...]
    unnamed x25 -> x19, local copies, waits for them, and re-layouts: 2.98 us -> 0.23 us
    ppermute x5, waiting for transfers between devices: 2.59 us -> 5.19 us  [ring(): lax.ppermute(value, axis, [(i, (i + 1) % count) for i in range(count)])]
    all_to_all x1, starting transfers between devices: 19.2 us -> 16.6 us  [local(): lax.all_to_all(boxes, 'video', split_axis=0, concat_axis=0, tiled=True)]
    slice x3 -> x1, local copies, waits for them, and re-layouts: 3.56 us -> 1.7 us  [local(): raw.append(jnp.swapaxes(features[0, turn], 1, 2))]
    pallas_call x2, Pallas kernels: 9.74 us -> 8.25 us  [decode(): pl.pallas_call(functools.partial(decode_kernel, joined), out_shape=jax.Sh...]
  transfers between devices with their start and end apart: 9 -> 9, of which waited for: 2 -> 2; matrix products, arithmetic and copies ran while one was open for 6% -> 2% of each run, Pallas kernels for 8% -> 9%
where the time goes in v3:
time: 89.7 us; the launch traced here: 90.2 us
  waiting for transfers between devices  43.6 us (49%)
  starting transfers between devices  28.4 us (32%)
  Pallas kernels  8.84 us (10%)
  local copies, waits for them, and re-layouts  4.78 us (5%)
  between operations  2.86 us (3%)
  other arithmetic  1.66 us (2%)
    all_to_all x1, waiting for transfers between devices, local(): lax.all_to_all(boxes, 'video', split_axis=0, concat_axis=0, tiled=True)  38.4 us
    all_to_all x1, starting transfers between devices, local(): lax.all_to_all(boxes, 'video', split_axis=0, concat_axis=0, tiled=True)  16.6 us
    pallas_call x2, Pallas kernels, decode(): pl.pallas_call(functools.partial(decode_kernel, joined), out_shape=jax.Sh...  8.25 us
    ppermute x3, starting transfers between devices, neighbours(): lax.ppermute(value, axis, [((i + 1) % lax.axis_size(axis), i) for i in ra...  6.46 us
    ppermute x5, starting transfers between devices, ring(): lax.ppermute(value, axis, [(i, (i + 1) % count) for i in range(count)])  5.35 us
    ppermute x5, waiting for transfers between devices, ring(): lax.ppermute(value, axis, [(i, (i + 1) % count) for i in range(count)])  5.19 us
  transfers between devices with their start and end apart: 9, of which 2 were waited for; matrix products, arithmetic and copies ran while one was open for 2% of the time, Pallas kernels for 9%

profile of v3, /device:TPU:1, one launch (start us, length us, event | category | flops | bytes accessed | tf_op | source)
XLA Modules:
  0.0 90.2 jit_solution(18116871274454682321)
XLA Ops:
  0.0 1.7 %fusion.20 = (bf16[1,1,8,96,2,128]{5,4,3,2,1,0:T(2,128)(2,1)S(1)}, bf16[1,1,8,96,2,128]{5,4,3,2,1,0:T(2,128)(2,1)S(1)}) fusion(bf16[1,2,8,96,2,128]{5,4,3,2,1,0:T(2,128)(2,1)} %param.9), kind=kLoop, calls=%fused_computation.42 | loop fusion | bytes 1572864 | tf_op jit(solution)/shard_map/slice | solution.py:209
  1.7 0.0 copy-start.2
  1.7 0.0 copy-start.7
  1.7 0.0 copy-start.4
  1.8 0.0 copy-start.5
  1.8 0.0 copy-start.6
  1.8 0.2 fusion
  2.0 0.0 copy-done.3
  2.0 0.5 fusion.15
  2.5 2.2 %collective-permute-start.2 = (bf16[8,2,96,128]{3,2,1,0:T(8,128)(2,1)S(1)}, bf16[8,2,96,128]{3,2,1,0:T(8,128)(2,1)S(1)}, u32[]{:S(2)}, u32[]{:S(2)}) collective-permute-start(bf16[8,2,96,128]{3,2,1,0:T(8,128)(2,1)S(1)} %get-tuple-element.28.rest_1_), channel_id=1, source_target_pairs={{0,1},{1,2},{2,3},{3,0},{4,5},{5,6},{6,7},{7,4},{8,9},{9,10},{10,1... | collective-permute-start | bytes 1179656 | tf_op jit(solution)/shard_map/ppermute | solution.py:29
  4.7 1.5 %collective-permute-start.3 = (bf16[8,2,96,128]{3,2,1,0:T(8,128)(2,1)S(1)}, bf16[8,2,96,128]{3,2,1,0:T(8,128)(2,1)S(1)}, u32[]{:S(2)}, u32[]{:S(2)}) collective-permute-start(bf16[8,2,96,128]{3,2,1,0:T(8,128)(2,1)S(1)} %get-tuple-element.28.rest_1_), channel_id=1, source_target_pairs={{1,0},{2,1},{3,2},{0,3},{5,4},{6,5},{7,6},{4,7},{9,8},{10,9},{11,1... | collective-permute-start | bytes 1179656 | tf_op jit(solution)/shard_map/ppermute | solution.py:33
  6.3 1.3 %collective-permute-start = (bf16[4,2,96,128]{3,2,1,0:T(8,128)(2,1)S(1)}, bf16[4,2,96,128]{3,2,1,0:T(8,128)(2,1)S(1)}, u32[]{:S(2)}, u32[]{:S(2)}) collective-permute-start(bf16[4,2,96,128]{3,2,1,0:T(8,128)(2,1)S(1)} %slice.26), channel_id=1, source_target_pairs={{0,4},{4,8},{8,12},{12,0},{1,5},{5,9},{9,13},{13,1},{2,6},{6,10},{... | collective-permute-start | bytes 589832 | tf_op jit(solution)/shard_map/ppermute | solution.py:29
  7.6 1.3 %collective-permute-start.1 = (bf16[4,2,96,128]{3,2,1,0:T(8,128)(2,1)S(1)}, bf16[4,2,96,128]{3,2,1,0:T(8,128)(2,1)S(1)}, u32[]{:S(2)}, u32[]{:S(2)}) collective-permute-start(bf16[4,2,96,128]{3,2,1,0:T(8,128)(2,1)S(1)} %slice.27), channel_id=1, source_target_pairs={{0,4},{4,8},{8,12},{12,0},{1,5},{5,9},{9,13},{13,1},{2,6},{6,10},{... | collective-permute-start | bytes 589832 | tf_op jit(solution)/shard_map/ppermute | solution.py:29
  8.9 0.0 copy-done.2
  8.9 0.1 copy.28
  9.0 0.2 divide_reduce_fusion
  9.2 0.2 fusion.19
  9.5 0.3 fusion.17
  9.8 0.0 copy-done.7
  9.8 0.6 dynamic_slice.12
  13.0 0.1 concatenate.7.flags
  13.1 0.1 concatenate.6.flags
  13.2 0.0 collective-permute-done.last.rest_4_
  13.2 0.1 broadcast_in_dim.18.gain_two
  13.3 0.1 broadcast_in_dim.19.bias_one
  13.4 0.1 broadcast_in_dim.20.bias_two
  13.5 0.0 copy-start.1
  13.5 0.1 collective-permute-start.6
  13.6 2.7 %collective-permute-start.7 = (bf16[4,2,96,128]{3,2,1,0:T(8,128)(2,1)S(1)}, bf16[4,2,96,128]{3,2,1,0:T(8,128)(2,1)S(1)}, u32[]{:S(2)}, u32[]{:S(2)}) collective-permute-start(bf16[4,2,96,128]{3,2,1,0:T(8,128)(2,1)S(1)} %collective-permute-done.last.rest_4_), channel_id=1, source_target_pairs={{1,0},{2,1},{3,2},{0,3},{5,4},{6,5},{7,6},{4,7},{9,8},{10,9},{11,1... | collective-permute-start | bytes 589832 | tf_op jit(solution)/shard_map/ppermute | solution.py:33
  16.2 0.0 collective-permute-done.1.past
  16.2 0.0 collective-permute-done.2.low.rest_2_
  16.2 0.0 collective-permute-done.3.high.rest_3_
  16.2 0.6 join.1.rest_1_.rest_4_
  16.8 0.5 collective-permute-start.4
  17.3 2.3 %collective-permute-start.5 = (bf16[12,2,96,128]{3,2,1,0:T(8,128)(2,1)S(1)}, bf16[12,2,96,128]{3,2,1,0:T(8,128)(2,1)S(1)}, u32[]{:S(2)}, u32[]{:S(2)}) collective-permute-start(bf16[12,2,96,128]{3,2,1,0:T(8,128)(2,1)S(1)} %join.1.rest_1_.rest_4_), channel_id=1, source_target_pairs={{1,0},{2,1},{3,2},{0,3},{5,4},{6,5},{7,6},{4,7},{9,8},{10,9},{11,1... | collective-permute-start | bytes 1769480 | tf_op jit(solution)/shard_map/ppermute | solution.py:33
  19.6 0.1 copy.44
  19.6 0.1 copy.43
  19.7 0.0 collective-permute-done.6.rest_5_
  19.7 0.0 collective-permute-done.7.rest_6_
  19.7 7.7 %decode.2.rest_9_ = bf16[16,2,2,96,128]{4,3,2,1,0:T(8,128)(2,1)} custom-call(s32[9]{0:T(128)S(1)} %concatenate.6.flags, f32[96,128]{1,0:T(8,128)S(1)} %broadcast_in_dim.18.gain_two, f32[96,128]{1,0:T(8,128)S(1)} %broadcast_in_dim.19.bias_one, f32[96,128]{1,0:T(8,128)S(1)} %broadcast_in_dim.20.bias_two, bf16[8,2,96,128]{3,2,1,0:T(8,128)(2,1)S(1)} %bitcast.36, ...), custom_call_target="tpu_custom_call" | custom-call | flops 6000000000 | bytes 4000000 | tf_op jit(solution)/shard_map/decode/pallas_call | solution.py:139
  27.4 5.2 %collective-permute-done.4.rest_2_.rest_5_ = bf16[12,2,96,128]{3,2,1,0:T(8,128)(2,1)S(1)} collective-permute-done((bf16[12,2,96,128]{3,2,1,0:T(8,128)(2,1)S(1)}, bf16[12,2,96,128]{3,2,1,0:T(8,128)(2,1)S(1)}, u32[]{:S(2)}, u32[]{:S(2)}) %collective-permute-start.4) | collective-permute-done | bytes 589856 | tf_op jit(solution)/shard_map/ppermute | solution.py:29
  32.6 0.0 collective-permute-done.5.rest_3_.rest_6_
  32.6 0.6 decode.3
  33.2 16.6 %all-to-all-start = ((bf16[16,2,2,96,128]{4,3,2,1,0:T(8,128)(2,1)}), bf16[16,2,2,96,128]{4,3,2,1,0:T(8,128)(2,1)S(1)}, u32[]{:S(2)}, u32[]{:S(2)}) async-start(bf16[16,2,2,96,128]{4,3,2,1,0:T(8,128)(2,1)} %decode.3), calls=%async_computation | async-start | bytes 3145728 | tf_op jit(solution)/shard_map/all_to_all | solution.py:246
  49.8 38.4 %all-to-all-done = bf16[16,2,2,96,128]{4,3,2,1,0:T(8,128)(2,1)S(1)} async-done(((bf16[16,2,2,96,128]{4,3,2,1,0:T(8,128)(2,1)}), bf16[16,2,2,96,128]{4,3,2,1,0:T(8,128)(2,1)S(1)}, u32[]{:S(2)}, u32[]{:S(2)}) %all-to-all-start) | async-done | bytes 1572896 | tf_op jit(solution)/shard_map/all_to_all | solution.py:246
  88.2 0.6 gather_fusion
  88.9 0.1 broadcast_select_fusion
  89.0 1.2 %copy.30 = bf16[1,10,96,2,128]{4,3,2,1,0:T(2,128)(2,1)} copy(bf16[1,10,96,2,128]{4,2,3,1,0:T(8,128)(2,1)S(1)} %bitcast.37) | data formatting | bytes 983040 | tf_op jit(solution)/shard_map/reshape | solution.py:249
  (17 shorter events, 0.1 us)
Async XLA Ops:
  0.0 2.0 %copy-start.3 = (f32[96]{0:T(128)S(1)}, f32[96]{0:T(128)}, u32[]{:S(2)}) copy-start(f32[96]{0:T(128)} %param.12) | copy-start | bytes 1156
  1.7 7.2 %copy-start.2 = (s32[16,32]{1,0:T(8,128)S(1)}, s32[16,32]{1,0:T(8,128)}, u32[]{:S(2)}) copy-start(s32[16,32]{1,0:T(8,128)} %param.11) | copy-start | bytes 6148
  1.7 8.1 %copy-start.7 = (s32[16]{0:T(128)S(1)}, s32[16]{0:T(128)}, u32[]{:S(2)}) copy-start(s32[16]{0:T(128)} %param.10) | copy-start | bytes 196
  1.7 11.5 %copy-start.4 = (f32[96]{0:T(128)S(1)}, f32[96]{0:T(128)}, u32[]{:S(2)}) copy-start(f32[96]{0:T(128)} %param.13) | copy-start | bytes 1156
  1.8 11.5 %copy-start.5 = (f32[96]{0:T(128)S(1)}, f32[96]{0:T(128)}, u32[]{:S(2)}) copy-start(f32[96]{0:T(128)} %param.16) | copy-start | bytes 1156
  1.8 11.6 %copy-start.6 = (f32[96]{0:T(128)S(1)}, f32[96]{0:T(128)}, u32[]{:S(2)}) copy-start(f32[96]{0:T(128)} %param.17) | copy-start | bytes 1156
  2.5 13.7 %collective-permute-start.2 = (bf16[8,2,96,128]{3,2,1,0:T(8,128)(2,1)S(1)}, bf16[8,2,96,128]{3,2,1,0:T(8,128)(2,1)S(1)}, u32[]{:S(2)}, u32[]{:S(2)}) collective-permute-start(bf16[8,2,96,128]{3,2,1,0:T(8,128)(2,1)S(1)} %get-tuple-element.28.rest_1_), channel_id=1, source_target_pairs={{0,1},{1,2},{2,3},{3,0},{4,5},{5,6},{6,7},{7,4},{8,9},{9,10},{10,1... | collective-permute-start | bytes 1179656 | tf_op jit(solution)/shard_map/ppermute | solution.py:29
  4.7 11.5 %collective-permute-start.3 = (bf16[8,2,96,128]{3,2,1,0:T(8,128)(2,1)S(1)}, bf16[8,2,96,128]{3,2,1,0:T(8,128)(2,1)S(1)}, u32[]{:S(2)}, u32[]{:S(2)}) collective-permute-start(bf16[8,2,96,128]{3,2,1,0:T(8,128)(2,1)S(1)} %get-tuple-element.28.rest_1_), channel_id=1, source_target_pairs={{1,0},{2,1},{3,2},{0,3},{5,4},{6,5},{7,6},{4,7},{9,8},{10,9},{11,1... | collective-permute-start | bytes 1179656 | tf_op jit(solution)/shard_map/ppermute | solution.py:33
  6.3 6.9 %collective-permute-start = (bf16[4,2,96,128]{3,2,1,0:T(8,128)(2,1)S(1)}, bf16[4,2,96,128]{3,2,1,0:T(8,128)(2,1)S(1)}, u32[]{:S(2)}, u32[]{:S(2)}) collective-permute-start(bf16[4,2,96,128]{3,2,1,0:T(8,128)(2,1)S(1)} %slice.26), channel_id=1, source_target_pairs={{0,4},{4,8},{8,12},{12,0},{1,5},{5,9},{9,13},{13,1},{2,6},{6,10},{... | collective-permute-start | bytes 589832 | tf_op jit(solution)/shard_map/ppermute | solution.py:29
  7.6 8.6 %collective-permute-start.1 = (bf16[4,2,96,128]{3,2,1,0:T(8,128)(2,1)S(1)}, bf16[4,2,96,128]{3,2,1,0:T(8,128)(2,1)S(1)}, u32[]{:S(2)}, u32[]{:S(2)}) collective-permute-start(bf16[4,2,96,128]{3,2,1,0:T(8,128)(2,1)S(1)} %slice.27), channel_id=1, source_target_pairs={{0,4},{4,8},{8,12},{12,0},{1,5},{5,9},{9,13},{13,1},{2,6},{6,10},{... | collective-permute-start | bytes 589832 | tf_op jit(solution)/shard_map/ppermute | solution.py:29
  13.5 6.3 %copy-start = (bf16[3,3,3,96,96]{4,3,2,1,0:T(8,128)(2,1)S(1)}, bf16[3,3,3,96,96]{4,3,2,1,0:T(8,128)(2,1)}, u32[]{:S(2)}) copy-start(bf16[3,3,3,96,96]{4,3,2,1,0:T(8,128)(2,1)} %rest_7_.3) | copy-start | bytes 1492996
  13.5 6.3 %copy-start.1 = (bf16[3,3,3,96,96]{4,3,2,1,0:T(8,128)(2,1)S(1)}, bf16[3,3,3,96,96]{4,3,2,1,0:T(8,128)(2,1)}, u32[]{:S(2)}) copy-start(bf16[3,3,3,96,96]{4,3,2,1,0:T(8,128)(2,1)} %rest_8_.3) | copy-start | bytes 1492996
  13.5 6.2 %collective-permute-start.6 = (bf16[4,2,96,128]{3,2,1,0:T(8,128)(2,1)S(1)}, bf16[4,2,96,128]{3,2,1,0:T(8,128)(2,1)S(1)}, u32[]{:S(2)}, u32[]{:S(2)}) collective-permute-start(bf16[4,2,96,128]{3,2,1,0:T(8,128)(2,1)S(1)} %collective-permute-done.last.rest_4_), channel_id=1, source_target_pairs={{0,1},{1,2},{2,3},{3,0},{4,5},{5,6},{6,7},{7,4},{8,9},{9,10},{10,1... | collective-permute-start | bytes 589832 | tf_op jit(solution)/shard_map/ppermute | solution.py:29
  13.6 6.2 %collective-permute-start.7 = (bf16[4,2,96,128]{3,2,1,0:T(8,128)(2,1)S(1)}, bf16[4,2,96,128]{3,2,1,0:T(8,128)(2,1)S(1)}, u32[]{:S(2)}, u32[]{:S(2)}) collective-permute-start(bf16[4,2,96,128]{3,2,1,0:T(8,128)(2,1)S(1)} %collective-permute-done.last.rest_4_), channel_id=1, source_target_pairs={{1,0},{2,1},{3,2},{0,3},{5,4},{6,5},{7,6},{4,7},{9,8},{10,9},{11,1... | collective-permute-start | bytes 589832 | tf_op jit(solution)/shard_map/ppermute | solution.py:33
  16.8 15.8 %collective-permute-start.4 = (bf16[12,2,96,128]{3,2,1,0:T(8,128)(2,1)S(1)}, bf16[12,2,96,128]{3,2,1,0:T(8,128)(2,1)S(1)}, u32[]{:S(2)}, u32[]{:S(2)}) collective-permute-start(bf16[12,2,96,128]{3,2,1,0:T(8,128)(2,1)S(1)} %join.1.rest_1_.rest_4_), channel_id=1, source_target_pairs={{0,1},{1,2},{2,3},{3,0},{4,5},{5,6},{6,7},{7,4},{8,9},{9,10},{10,1... | collective-permute-start | bytes 1769480 | tf_op jit(solution)/shard_map/ppermute | solution.py:29
  17.3 15.3 %collective-permute-start.5 = (bf16[12,2,96,128]{3,2,1,0:T(8,128)(2,1)S(1)}, bf16[12,2,96,128]{3,2,1,0:T(8,128)(2,1)S(1)}, u32[]{:S(2)}, u32[]{:S(2)}) collective-permute-start(bf16[12,2,96,128]{3,2,1,0:T(8,128)(2,1)S(1)} %join.1.rest_1_.rest_4_), channel_id=1, source_target_pairs={{1,0},{2,1},{3,2},{0,3},{5,4},{6,5},{7,6},{4,7},{9,8},{10,9},{11,1... | collective-permute-start | bytes 1769480 | tf_op jit(solution)/shard_map/ppermute | solution.py:33
  33.2 55.0 %all-to-all-start = ((bf16[16,2,2,96,128]{4,3,2,1,0:T(8,128)(2,1)}), bf16[16,2,2,96,128]{4,3,2,1,0:T(8,128)(2,1)S(1)}, u32[]{:S(2)}, u32[]{:S(2)}) async-start(bf16[16,2,2,96,128]{4,3,2,1,0:T(8,128)(2,1)} %decode.3), calls=%async_computation | async-start | bytes 3145728 | tf_op jit(solution)/shard_map/all_to_all | solution.py:246

commit v4 on v3

--- a/solution.py
+++ b/solution.py
@@ -44,19 +44,30 @@
         stack[start : start + C, columns] = shifted
 
 
-def multiply(weights, stack, row, frame):
-    total = None
-    for tap in range(3):
-        window = stack[row * TAPS : (row + 4) * TAPS, (frame + tap) * W : (frame + tap + 2) * W]
-        part = jnp.dot(weights[tap], window, preferred_element_type=jnp.float32)
-        total = part if total is None else total + part
-    return total
+def convolve(weights, stack, row, frames, sums):
+    last = frames // 2
+    for pair in range(last + 1):
+        window = stack[row * TAPS : (row + 3) * TAPS, 2 * pair * W : (2 * pair + 2) * W]
+        low, high = (0 if pair < last else 1), (3 if pair > 0 else 2)
+        parts = jnp.dot(
+            weights[low * C : high * C, :], window, preferred_element_type=jnp.float32
+        )
+        parts = {tap: parts[(tap - low) * C :][:C] for tap in range(low, high)}
+        if 0 in parts:
+            sums[row, :, 2 * pair * W : (2 * pair + 2) * W] = parts[0]
+        for j in range(2):
+            frame = 2 * pair + j - 1
+            if 0 <= frame < frames:
+                columns = slice(frame * W, (frame + 1) * W)
+                sums[row, :, columns] = sums[row, :, columns] + parts[1][:, j * W : (j + 1) * W]
+        if 2 in parts:
+            yield 2 * pair - 2, sums[row, :, (2 * pair - 2) * W : 2 * pair * W] + parts[2]
 
 
 def decode_kernel(joined, flags, gain_two, bias_one, bias_two, *rest):
     arrays, rest = rest[:9], rest[9:]
     raw, own, low, high, tail, low_tail, high_tail, *plain = arrays
-    boxes, first, second, done, weights_one, weights_two, stores = rest[-7:]
+    boxes, first, second, sums, done, weights_one, weights_two, stores = rest[-8:]
     skip = SEG if joined else 0
 
     @pl.when(flags[0] > 0)
@@ -69,57 +80,68 @@
         above = flags[2] > 0
         below = flags[3] > 0
         zero = jnp.zeros((), jnp.bfloat16)
-        pair_weights(plain[0], weights_one)
-        for frames, base, start, parts in (
-            (TAIL, 0, skip, (tail, low_tail, high_tail)),
-            (SEG, TAIL, 0, (own, low, high)),
-        ):
-            known = True if base > 0 else past
-            for frame in range(frames):
-                for row in range(2):
-                    values = jnp.where(known, parts[0][start + frame, row], zero)
-                    spread(values, masks, first, 2 + row, base + frame)
-                    keep = jnp.logical_and(known, above)
-                    values = jnp.where(keep, parts[1][start + frame, row], zero)
-                    spread(values, masks, first, row, base + frame)
-                    keep = jnp.logical_and(known, below)
-                    values = jnp.where(keep, parts[2][start + frame, row], zero)
-                    spread(values, masks, first, 4 + row, base + frame)
+        lay_out(plain[0], weights_one)
+        def fill(row):
+            part, at = row // 2, row % 2
+            side = {0: above, 2: below}.get(part)
+            for frame in range(TAIL + SEG):
+                if frame < TAIL:
+                    values = (low_tail, tail, high_tail)[part][skip + frame, at]
+                    keep = past
+                else:
+                    values = (low, own, high)[part][frame - TAIL, at]
+                    keep = None
+                if side is not None:
+                    keep = side if keep is None else jnp.logical_and(keep, side)
+                if keep is not None:
+                    values = jnp.where(keep, values, zero)
+                spread(values, masks, first, row, frame)
+
         gain = gain_two[...]
-        offset = bias_one[...]
-        for row in range(0, 4, 2):
-            for frame in range(0, SEG + 2, 2):
-                total = multiply(weights_one, first, row, frame)
-                for k in range(2):
-                    for j in range(2):
-                        part = total[k * C : (k + 1) * C, j * W : (j + 1) * W] + offset
-                        part = part.astype(jnp.bfloat16).astype(jnp.float32)
-                        part = activate(part, gain, 0)
-                        keep = past if frame < 2 else None
-                        side = {0: above, 3: below}.get(row + k)
-                        if side is not None:
-                            keep = side if keep is None else jnp.logical_and(keep, side)
-                        if keep is not None:
-                            part = jnp.where(keep, part, 0.0)
-                        spread(part.astype(jnp.bfloat16), masks, second, row + k, frame + j)
-        pair_weights(plain[1], weights_two)
-        offset = bias_two[...]
+        offset_one = bias_one[...]
+        offset_two = bias_two[...]
+
+        def inner(row):
+            for frame, total in convolve(weights_one, first, row, SEG + 2, sums):
+                for j in range(2):
+                    part = total[:, j * W : (j + 1) * W] + offset_one
+                    part = part.astype(jnp.bfloat16).astype(jnp.float32)
+                    part = activate(part, gain, 0)
+                    keep = past if frame < 2 else None
+                    side = {0: above, 3: below}.get(row)
+                    if side is not None:
+                        keep = side if keep is None else jnp.logical_and(keep, side)
+                    if keep is not None:
+                        part = jnp.where(keep, part, 0.0)
+                    spread(part.astype(jnp.bfloat16), masks, second, row, frame + j)
 
         def store(block):
             return pltpu.make_async_copy(
                 done.at[block], boxes.at[flags[5 + block]], stores.at[block]
             )
 
-        for block in range(RB):
-            total = multiply(weights_two, second, 0, block * BF)
-            for j in range(BF):
-                frame = block * BF + j
-                for k in range(2):
-                    part = total[k * C : (k + 1) * C, j * W : (j + 1) * W] + offset
-                    part = part + raw[frame, k].astype(jnp.float32)
-                    part = jnp.where(frame < flags[4], part, 0.0)
-                    done[block, j, k] = part.astype(jnp.bfloat16)
-            store(block).start()
+        def outer(row):
+            for start, total in convolve(weights_two, second, row, SEG, sums):
+                for j in range(BF):
+                    part = total[:, j * W : (j + 1) * W] + offset_two
+                    part = part + raw[start + j, row].astype(jnp.float32)
+                    part = jnp.where(start + j < flags[4], part, 0.0)
+                    done[start // BF, j, row] = part.astype(jnp.bfloat16)
+                if row == 1:
+                    store(start // BF).start()
+
+        for row in range(3):
+            fill(row)
+        inner(0)
+        fill(3)
+        inner(1)
+        fill(4)
+        lay_out(plain[1], weights_two)
+        inner(2)
+        fill(5)
+        outer(0)
+        inner(3)
+        outer(1)
         for block in range(RB):
             store(block).wait()
 
@@ -135,7 +157,7 @@
         aliases = {len(operands): 0}
         operands.append(boxes)
         specs.append(pl.BlockSpec(memory_space=pl.ANY))
-    paired = pltpu.VMEM((3, 2 * C, 4 * TAPS), jnp.bfloat16)
+    taps = pltpu.VMEM((3 * C, 3 * TAPS), jnp.bfloat16)
     return pl.pallas_call(
         functools.partial(decode_kernel, joined),
         out_shape=jax.ShapeDtypeStruct((box_count, BF, 2, C, W), jnp.bfloat16),
@@ -144,9 +166,10 @@
         scratch_shapes=[
             pltpu.VMEM((6 * TAPS, (TAIL + SEG) * W), jnp.bfloat16),
             pltpu.VMEM((4 * TAPS, (2 + SEG) * W), jnp.bfloat16),
+            pltpu.VMEM((4, C, (2 + SEG) * W), jnp.float32),
             pltpu.VMEM((RB, BF, 2, C, W), jnp.bfloat16),
-            paired,
-            paired,
+            taps,
+            taps,
             pltpu.SemaphoreType.DMA((RB,)),
         ],
         input_output_aliases=aliases,
@@ -156,16 +179,12 @@
     )(*operands)
 
 
-def pair_weights(weight, pair):
-    pair[:, :C, 3 * TAPS :] = jnp.zeros((3, C, TAPS), jnp.bfloat16)
-    pair[:, C:, :TAPS] = jnp.zeros((3, C, TAPS), jnp.bfloat16)
+def lay_out(weight, rows):
     for tap in range(3):
         for row in range(3):
             for cell in range(3):
-                tile = weight[tap, row, cell]
-                for k in range(2):
-                    start = ((row + k) * 3 + cell) * C
-                    pair[tap, k * C : (k + 1) * C, start : start + C] = tile
+                start = (row * 3 + cell) * C
+                rows[tap * C : (tap + 1) * C, start : start + C] = weight[tap, row, cell]
 
 
 def join_kernel(flags, own, last, past, low, high, joined):

time: 89.7 us -> 87.1 us (0.971)
  starting transfers between devices: 28.4 us -> 25.4 us
    all_to_all x1, starting transfers between devices: 16.6 us -> 13.6 us  [local(): lax.all_to_all(boxes, 'video', split_axis=0, concat_axis=0, tiled=True)]
where the time goes in v4:
time: 87.1 us; the launch traced here: 87.2 us
  waiting for transfers between devices  44.4 us (51%)
  starting transfers between devices  25.4 us (29%)
  Pallas kernels  8.04 us (9%)
  local copies, waits for them, and re-layouts  4.78 us (5%)
  between operations  2.86 us (3%)
  other arithmetic  1.66 us (2%)
    all_to_all x1, waiting for transfers between devices, local(): lax.all_to_all(boxes, 'video', split_axis=0, concat_axis=0, tiled=True)  38.4 us
    all_to_all x1, starting transfers between devices, local(): lax.all_to_all(boxes, 'video', split_axis=0, concat_axis=0, tiled=True)  13.6 us
    pallas_call x2, Pallas kernels, decode(): pl.pallas_call(functools.partial(decode_kernel, joined), out_shape=jax.Sh...  7.45 us
    ppermute x3, starting transfers between devices, neighbours(): lax.ppermute(value, axis, [((i + 1) % lax.axis_size(axis), i) for i in ra...  6.46 us
    ppermute x5, waiting for transfers between devices, ring(): lax.ppermute(value, axis, [(i, (i + 1) % count) for i in range(count)])  6 us
    ppermute x5, starting transfers between devices, ring(): lax.ppermute(value, axis, [(i, (i + 1) % count) for i in range(count)])  5.35 us
  transfers between devices with their start and end apart: 9, of which 2 were waited for; matrix products, arithmetic and copies ran while one was open for 2% of the time, Pallas kernels for 9%

profile of v4, /device:TPU:1, one launch (start us, length us, event | category | flops | bytes accessed | tf_op | source)
XLA Modules:
  0.0 87.2 jit_solution(10894416952001365050)
XLA Ops:
  0.0 1.7 %fusion.20 = (bf16[1,1,8,96,2,128]{5,4,3,2,1,0:T(2,128)(2,1)S(1)}, bf16[1,1,8,96,2,128]{5,4,3,2,1,0:T(2,128)(2,1)S(1)}) fusion(bf16[1,2,8,96,2,128]{5,4,3,2,1,0:T(2,128)(2,1)} %param.9), kind=kLoop, calls=%fused_computation.42 | loop fusion | bytes 1572864 | tf_op jit(solution)/shard_map/slice | solution.py:228
  1.7 0.0 copy-start.2
  1.7 0.0 copy-start.7
  1.7 0.0 copy-start.4
  1.8 0.0 copy-start.5
  1.8 0.0 copy-start.6
  1.8 0.2 fusion
  2.0 0.5 fusion.15
  2.5 2.2 %collective-permute-start.2 = (bf16[8,2,96,128]{3,2,1,0:T(8,128)(2,1)S(1)}, bf16[8,2,96,128]{3,2,1,0:T(8,128)(2,1)S(1)}, u32[]{:S(2)}, u32[]{:S(2)}) collective-permute-start(bf16[8,2,96,128]{3,2,1,0:T(8,128)(2,1)S(1)} %get-tuple-element.28.rest_1_), channel_id=1, source_target_pairs={{0,1},{1,2},{2,3},{3,0},{4,5},{5,6},{6,7},{7,4},{8,9},{9,10},{10,1... | collective-permute-start | bytes 1179656 | tf_op jit(solution)/shard_map/ppermute | solution.py:29
  4.7 1.5 %collective-permute-start.3 = (bf16[8,2,96,128]{3,2,1,0:T(8,128)(2,1)S(1)}, bf16[8,2,96,128]{3,2,1,0:T(8,128)(2,1)S(1)}, u32[]{:S(2)}, u32[]{:S(2)}) collective-permute-start(bf16[8,2,96,128]{3,2,1,0:T(8,128)(2,1)S(1)} %get-tuple-element.28.rest_1_), channel_id=1, source_target_pairs={{1,0},{2,1},{3,2},{0,3},{5,4},{6,5},{7,6},{4,7},{9,8},{10,9},{11,1... | collective-permute-start | bytes 1179656 | tf_op jit(solution)/shard_map/ppermute | solution.py:33
  6.3 1.3 %collective-permute-start = (bf16[4,2,96,128]{3,2,1,0:T(8,128)(2,1)S(1)}, bf16[4,2,96,128]{3,2,1,0:T(8,128)(2,1)S(1)}, u32[]{:S(2)}, u32[]{:S(2)}) collective-permute-start(bf16[4,2,96,128]{3,2,1,0:T(8,128)(2,1)S(1)} %slice.26), channel_id=1, source_target_pairs={{0,4},{4,8},{8,12},{12,0},{1,5},{5,9},{9,13},{13,1},{2,6},{6,10},{... | collective-permute-start | bytes 589832 | tf_op jit(solution)/shard_map/ppermute | solution.py:29
  7.6 1.3 %collective-permute-start.1 = (bf16[4,2,96,128]{3,2,1,0:T(8,128)(2,1)S(1)}, bf16[4,2,96,128]{3,2,1,0:T(8,128)(2,1)S(1)}, u32[]{:S(2)}, u32[]{:S(2)}) collective-permute-start(bf16[4,2,96,128]{3,2,1,0:T(8,128)(2,1)S(1)} %slice.27), channel_id=1, source_target_pairs={{0,4},{4,8},{8,12},{12,0},{1,5},{5,9},{9,13},{13,1},{2,6},{6,10},{... | collective-permute-start | bytes 589832 | tf_op jit(solution)/shard_map/ppermute | solution.py:29
  8.9 0.1 copy.28
  9.0 0.2 divide_reduce_fusion
  9.2 0.2 fusion.19
  9.5 0.3 fusion.17
  9.8 0.6 dynamic_slice.12
  13.0 0.1 concatenate.7.flags
  13.1 0.1 concatenate.6.flags
  13.2 0.0 collective-permute-done.last.rest_4_
  13.2 0.0 copy-done.4
  13.2 0.1 broadcast_in_dim.18.gain_two
  13.3 0.0 copy-done.5
  13.3 0.1 broadcast_in_dim.19.bias_one
  13.4 0.0 copy-done.6
  13.4 0.1 broadcast_in_dim.20.bias_two
  13.5 0.0 copy-start.1
  13.5 0.1 collective-permute-start.6
  13.6 2.7 %collective-permute-start.7 = (bf16[4,2,96,128]{3,2,1,0:T(8,128)(2,1)S(1)}, bf16[4,2,96,128]{3,2,1,0:T(8,128)(2,1)S(1)}, u32[]{:S(2)}, u32[]{:S(2)}) collective-permute-start(bf16[4,2,96,128]{3,2,1,0:T(8,128)(2,1)S(1)} %collective-permute-done.last.rest_4_), channel_id=1, source_target_pairs={{1,0},{2,1},{3,2},{0,3},{5,4},{6,5},{7,6},{4,7},{9,8},{10,9},{11,1... | collective-permute-start | bytes 589832 | tf_op jit(solution)/shard_map/ppermute | solution.py:33
  16.2 0.0 collective-permute-done.1.past
  16.2 0.0 collective-permute-done.2.low.rest_2_
  16.2 0.0 collective-permute-done.3.high.rest_3_
  16.2 0.6 join.1.rest_1_.rest_4_
  16.8 0.5 collective-permute-start.4
  17.3 2.3 %collective-permute-start.5 = (bf16[12,2,96,128]{3,2,1,0:T(8,128)(2,1)S(1)}, bf16[12,2,96,128]{3,2,1,0:T(8,128)(2,1)S(1)}, u32[]{:S(2)}, u32[]{:S(2)}) collective-permute-start(bf16[12,2,96,128]{3,2,1,0:T(8,128)(2,1)S(1)} %join.1.rest_1_.rest_4_), channel_id=1, source_target_pairs={{1,0},{2,1},{3,2},{0,3},{5,4},{6,5},{7,6},{4,7},{9,8},{10,9},{11,1... | collective-permute-start | bytes 1769480 | tf_op jit(solution)/shard_map/ppermute | solution.py:33
  19.6 0.1 copy.44
  19.6 0.1 copy.43
  19.7 0.0 collective-permute-done.6.rest_5_
  19.7 0.0 collective-permute-done.7.rest_6_
  19.7 6.9 %decode.2.rest_9_ = bf16[16,2,2,96,128]{4,3,2,1,0:T(8,128)(2,1)} custom-call(s32[9]{0:T(128)S(1)} %concatenate.6.flags, f32[96,128]{1,0:T(8,128)S(1)} %broadcast_in_dim.18.gain_two, f32[96,128]{1,0:T(8,128)S(1)} %broadcast_in_dim.19.bias_one, f32[96,128]{1,0:T(8,128)S(1)} %broadcast_in_dim.20.bias_two, bf16[8,2,96,128]{3,2,1,0:T(8,128)(2,1)S(1)} %bitcast.36, ...), custom_call_target="tpu_custom_call" | custom-call | flops 6000000000 | bytes 4000000 | tf_op jit(solution)/shard_map/decode/pallas_call | solution.py:161
  26.6 6.0 %collective-permute-done.4.rest_2_.rest_5_ = bf16[12,2,96,128]{3,2,1,0:T(8,128)(2,1)S(1)} collective-permute-done((bf16[12,2,96,128]{3,2,1,0:T(8,128)(2,1)S(1)}, bf16[12,2,96,128]{3,2,1,0:T(8,128)(2,1)S(1)}, u32[]{:S(2)}, u32[]{:S(2)}) %collective-permute-start.4) | collective-permute-done | bytes 589856 | tf_op jit(solution)/shard_map/ppermute | solution.py:29
  32.6 0.0 collective-permute-done.5.rest_3_.rest_6_
  32.6 0.6 decode.3
  33.2 13.6 %all-to-all-start = ((bf16[16,2,2,96,128]{4,3,2,1,0:T(8,128)(2,1)}), bf16[16,2,2,96,128]{4,3,2,1,0:T(8,128)(2,1)S(1)}, u32[]{:S(2)}, u32[]{:S(2)}) async-start(bf16[16,2,2,96,128]{4,3,2,1,0:T(8,128)(2,1)} %decode.3), calls=%async_computation | async-start | bytes 3145728 | tf_op jit(solution)/shard_map/all_to_all | solution.py:265
  46.8 38.4 %all-to-all-done = bf16[16,2,2,96,128]{4,3,2,1,0:T(8,128)(2,1)S(1)} async-done(((bf16[16,2,2,96,128]{4,3,2,1,0:T(8,128)(2,1)}), bf16[16,2,2,96,128]{4,3,2,1,0:T(8,128)(2,1)S(1)}, u32[]{:S(2)}, u32[]{:S(2)}) %all-to-all-start) | async-done | bytes 1572896 | tf_op jit(solution)/shard_map/all_to_all | solution.py:265
  85.2 0.6 gather_fusion
  85.9 0.1 broadcast_select_fusion
  86.0 1.2 %copy.30 = bf16[1,10,96,2,128]{4,3,2,1,0:T(2,128)(2,1)} copy(bf16[1,10,96,2,128]{4,2,3,1,0:T(8,128)(2,1)S(1)} %bitcast.37) | data formatting | bytes 983040 | tf_op jit(solution)/shard_map/reshape | solution.py:268
  (17 shorter events, 0.1 us)
Async XLA Ops:
  0.0 2.0 %copy-start.3 = (f32[96]{0:T(128)S(1)}, f32[96]{0:T(128)}, u32[]{:S(2)}) copy-start(f32[96]{0:T(128)} %param.12) | copy-start | bytes 1156
  1.7 7.2 %copy-start.2 = (s32[16,32]{1,0:T(8,128)S(1)}, s32[16,32]{1,0:T(8,128)}, u32[]{:S(2)}) copy-start(s32[16,32]{1,0:T(8,128)} %param.11) | copy-start | bytes 6148
  1.7 8.1 %copy-start.7 = (s32[16]{0:T(128)S(1)}, s32[16]{0:T(128)}, u32[]{:S(2)}) copy-start(s32[16]{0:T(128)} %param.10) | copy-start | bytes 196
  1.7 11.5 %copy-start.4 = (f32[96]{0:T(128)S(1)}, f32[96]{0:T(128)}, u32[]{:S(2)}) copy-start(f32[96]{0:T(128)} %param.13) | copy-start | bytes 1156
  1.8 11.5 %copy-start.5 = (f32[96]{0:T(128)S(1)}, f32[96]{0:T(128)}, u32[]{:S(2)}) copy-start(f32[96]{0:T(128)} %param.16) | copy-start | bytes 1156
  1.8 11.6 %copy-start.6 = (f32[96]{0:T(128)S(1)}, f32[96]{0:T(128)}, u32[]{:S(2)}) copy-start(f32[96]{0:T(128)} %param.17) | copy-start | bytes 1156
  2.5 13.7 %collective-permute-start.2 = (bf16[8,2,96,128]{3,2,1,0:T(8,128)(2,1)S(1)}, bf16[8,2,96,128]{3,2,1,0:T(8,128)(2,1)S(1)}, u32[]{:S(2)}, u32[]{:S(2)}) collective-permute-start(bf16[8,2,96,128]{3,2,1,0:T(8,128)(2,1)S(1)} %get-tuple-element.28.rest_1_), channel_id=1, source_target_pairs={{0,1},{1,2},{2,3},{3,0},{4,5},{5,6},{6,7},{7,4},{8,9},{9,10},{10,1... | collective-permute-start | bytes 1179656 | tf_op jit(solution)/shard_map/ppermute | solution.py:29
  4.7 11.5 %collective-permute-start.3 = (bf16[8,2,96,128]{3,2,1,0:T(8,128)(2,1)S(1)}, bf16[8,2,96,128]{3,2,1,0:T(8,128)(2,1)S(1)}, u32[]{:S(2)}, u32[]{:S(2)}) collective-permute-start(bf16[8,2,96,128]{3,2,1,0:T(8,128)(2,1)S(1)} %get-tuple-element.28.rest_1_), channel_id=1, source_target_pairs={{1,0},{2,1},{3,2},{0,3},{5,4},{6,5},{7,6},{4,7},{9,8},{10,9},{11,1... | collective-permute-start | bytes 1179656 | tf_op jit(solution)/shard_map/ppermute | solution.py:33
  6.3 6.9 %collective-permute-start = (bf16[4,2,96,128]{3,2,1,0:T(8,128)(2,1)S(1)}, bf16[4,2,96,128]{3,2,1,0:T(8,128)(2,1)S(1)}, u32[]{:S(2)}, u32[]{:S(2)}) collective-permute-start(bf16[4,2,96,128]{3,2,1,0:T(8,128)(2,1)S(1)} %slice.26), channel_id=1, source_target_pairs={{0,4},{4,8},{8,12},{12,0},{1,5},{5,9},{9,13},{13,1},{2,6},{6,10},{... | collective-permute-start | bytes 589832 | tf_op jit(solution)/shard_map/ppermute | solution.py:29
  7.6 8.6 %collective-permute-start.1 = (bf16[4,2,96,128]{3,2,1,0:T(8,128)(2,1)S(1)}, bf16[4,2,96,128]{3,2,1,0:T(8,128)(2,1)S(1)}, u32[]{:S(2)}, u32[]{:S(2)}) collective-permute-start(bf16[4,2,96,128]{3,2,1,0:T(8,128)(2,1)S(1)} %slice.27), channel_id=1, source_target_pairs={{0,4},{4,8},{8,12},{12,0},{1,5},{5,9},{9,13},{13,1},{2,6},{6,10},{... | collective-permute-start | bytes 589832 | tf_op jit(solution)/shard_map/ppermute | solution.py:29
  13.5 6.3 %copy-start = (bf16[3,3,3,96,96]{4,3,2,1,0:T(8,128)(2,1)S(1)}, bf16[3,3,3,96,96]{4,3,2,1,0:T(8,128)(2,1)}, u32[]{:S(2)}) copy-start(bf16[3,3,3,96,96]{4,3,2,1,0:T(8,128)(2,1)} %rest_7_.3) | copy-start | bytes 1492996
  13.5 6.3 %copy-start.1 = (bf16[3,3,3,96,96]{4,3,2,1,0:T(8,128)(2,1)S(1)}, bf16[3,3,3,96,96]{4,3,2,1,0:T(8,128)(2,1)}, u32[]{:S(2)}) copy-start(bf16[3,3,3,96,96]{4,3,2,1,0:T(8,128)(2,1)} %rest_8_.3) | copy-start | bytes 1492996
  13.5 6.2 %collective-permute-start.6 = (bf16[4,2,96,128]{3,2,1,0:T(8,128)(2,1)S(1)}, bf16[4,2,96,128]{3,2,1,0:T(8,128)(2,1)S(1)}, u32[]{:S(2)}, u32[]{:S(2)}) collective-permute-start(bf16[4,2,96,128]{3,2,1,0:T(8,128)(2,1)S(1)} %collective-permute-done.last.rest_4_), channel_id=1, source_target_pairs={{0,1},{1,2},{2,3},{3,0},{4,5},{5,6},{6,7},{7,4},{8,9},{9,10},{10,1... | collective-permute-start | bytes 589832 | tf_op jit(solution)/shard_map/ppermute | solution.py:29
  13.6 6.2 %collective-permute-start.7 = (bf16[4,2,96,128]{3,2,1,0:T(8,128)(2,1)S(1)}, bf16[4,2,96,128]{3,2,1,0:T(8,128)(2,1)S(1)}, u32[]{:S(2)}, u32[]{:S(2)}) collective-permute-start(bf16[4,2,96,128]{3,2,1,0:T(8,128)(2,1)S(1)} %collective-permute-done.last.rest_4_), channel_id=1, source_target_pairs={{1,0},{2,1},{3,2},{0,3},{5,4},{6,5},{7,6},{4,7},{9,8},{10,9},{11,1... | collective-permute-start | bytes 589832 | tf_op jit(solution)/shard_map/ppermute | solution.py:33
  16.8 15.8 %collective-permute-start.4 = (bf16[12,2,96,128]{3,2,1,0:T(8,128)(2,1)S(1)}, bf16[12,2,96,128]{3,2,1,0:T(8,128)(2,1)S(1)}, u32[]{:S(2)}, u32[]{:S(2)}) collective-permute-start(bf16[12,2,96,128]{3,2,1,0:T(8,128)(2,1)S(1)} %join.1.rest_1_.rest_4_), channel_id=1, source_target_pairs={{0,1},{1,2},{2,3},{3,0},{4,5},{5,6},{6,7},{7,4},{8,9},{9,10},{10,1... | collective-permute-start | bytes 1769480 | tf_op jit(solution)/shard_map/ppermute | solution.py:29
  17.3 15.3 %collective-permute-start.5 = (bf16[12,2,96,128]{3,2,1,0:T(8,128)(2,1)S(1)}, bf16[12,2,96,128]{3,2,1,0:T(8,128)(2,1)S(1)}, u32[]{:S(2)}, u32[]{:S(2)}) collective-permute-start(bf16[12,2,96,128]{3,2,1,0:T(8,128)(2,1)S(1)} %join.1.rest_1_.rest_4_), channel_id=1, source_target_pairs={{1,0},{2,1},{3,2},{0,3},{5,4},{6,5},{7,6},{4,7},{9,8},{10,9},{11,1... | collective-permute-start | bytes 1769480 | tf_op jit(solution)/shard_map/ppermute | solution.py:33
  33.2 52.0 %all-to-all-start = ((bf16[16,2,2,96,128]{4,3,2,1,0:T(8,128)(2,1)}), bf16[16,2,2,96,128]{4,3,2,1,0:T(8,128)(2,1)S(1)}, u32[]{:S(2)}, u32[]{:S(2)}) async-start(bf16[16,2,2,96,128]{4,3,2,1,0:T(8,128)(2,1)} %decode.3), calls=%async_computation | async-start | bytes 3145728 | tf_op jit(solution)/shard_map/all_to_all | solution.py:265
